TPU v7x, 256 devices: a whole 4x4x8 slice. The times are simulated.
256 devices in a mesh: pipe: 8 (over x, y_hi), ctx: 32 (over y_lo, z, core).
Axes of the slice: x: 4, y: 4 (y_hi: 2, y_lo: 2; y = y_hi * 2 + y_lo), z: 8, core: 2. Of those that a mesh axis runs over, the one named last changes fastest.
Arguments:
- stored_acts: bfloat16 [8, 4096, 1024], P('pipe', 'ctx'), may hold values from -6 to 6
- queries: bfloat16 [8, 4096, 1024], P('pipe', 'ctx'), may hold values from -40 to 40
- patch_times: int32 [8, 4096], P('pipe', 'ctx'), may hold values from 0 to 31, as said below
- key_gain: float32 [8, 1024], P('pipe'), may hold values from 0.5 to 2
- value_gain: float32 [8, 1024], P('pipe'), may hold values from 0.5 to 2
- conv_weight: bfloat16 [8, 27, 128, 128], P('pipe'), may hold values from -0.109375 to 0.109375
- prior_grad: bfloat16 [8, 4096, 1024], P('pipe', 'ctx'), may hold values from -6 to 6
- loss_grad: bfloat16 [4096, 1024], P('ctx'), may hold values from -6 to 6
Outputs:
- input_grad: bfloat16 [8, 4096, 1024], P('pipe', 'ctx')
Inputs may be any that keep to these rules, and one draw needn't show every extreme that they name: `patch_times`: within each aligned group of four patches of a sequence, no patch has a later time step than the first of the group.
All inputs are finite; a program needn't handle non-finite values.
Results may differ from a plain program's by a relative error of at most 0.012.
Values may be sent and summed in bfloat16 or wider, within the bound.
No kernel may reach another device: no remote copies, remote signals or barrier semaphores. Data moves between devices by JAX's collectives and lax.ppermute only.
A program may use at most 128 MiB of HBM per device.

v0:
```python
import math

import jax
import jax.numpy as jnp
from jax import lax
from jax.sharding import PartitionSpec as P

HEADS = 16
HEAD_DIM = 64
CHANNELS = 128
GY = 8
GZ = 8
D = 1024
FIELDS = 8


def shifted(value, axis, steps):
    count = lax.axis_size(axis)
    leading, last = (max(0, -steps), min(count, count - steps))
    return lax.ppermute(value, axis, [(source, source + steps) for source in range(leading, last)])


def padded_2(block, sides, width):
    for axis, dim in sides:
        count = lax.axis_size(axis)
        forward = [(i, i + 1) for i in range(count - 1)]
        backward = [(target, source) for source, target in forward]
        low = lax.ppermute(
            lax.slice_in_dim(block, block.shape[dim] - width, None, axis=dim), axis, forward
        )
        high = lax.ppermute(lax.slice_in_dim(block, 0, width, axis=dim), axis, backward)
        block = jnp.concatenate([low, block, high], axis=dim)
    return block


def conv_backward(extended, weight, row_count):
    planes = row_count // (GY * GZ)
    grid_field = extended.reshape(planes + 2, GY, GZ, FIELDS, CHANNELS)
    padded = jnp.pad(grid_field, ((0, 0), (1, 1), (1, 1), (0, 0), (0, 0)))
    windows = []
    for shift_x in (-1, 0, 1):
        for shift_y in (-1, 0, 1):
            for shift_z in (-1, 0, 1):
                windows.append(
                    padded[
                        1 - shift_x : 1 - shift_x + planes,
                        1 - shift_y : 1 - shift_y + GY,
                        1 - shift_z : 1 - shift_z + GZ,
                    ]
                )
    stacked = jnp.stack(windows, axis=4).reshape(row_count * FIELDS, 27 * CHANNELS)
    matrix = jnp.transpose(weight, (0, 2, 1)).reshape(27 * CHANNELS, CHANNELS)
    return jnp.dot(stacked, matrix, preferred_element_type=jnp.float32).reshape(row_count, D)


def split_heads(matrix):
    return matrix.reshape(matrix.shape[0], HEADS, matrix.shape[1] // HEADS)


def keys_values(rows_x, key_scale, value_scale):
    widened = rows_x.astype(jnp.float32)
    keyed = split_heads((widened * key_scale).astype(jnp.bfloat16))
    valued = jnp.roll(split_heads((widened * value_scale).astype(jnp.bfloat16)), HEADS // 2, axis=1)
    return (keyed, valued)


def masked_scores(query_heads, key_heads, query_times, key_times):
    scores = jnp.einsum(
        "qhe,khe->qhk", query_heads, key_heads, preferred_element_type=jnp.float32
    ) * HEAD_DIM ** (-0.5)
    visible = key_times[None, None, :] <= query_times[:, None, None]
    return jnp.where(visible, scores, -jnp.inf)


def running_stats(running, query_heads, grad_heads, query_times, key_heads, value_heads, key_times):
    running_max, running_sum, weighted = running
    scores = masked_scores(query_heads, key_heads, query_times, key_times)
    prob_grad = jnp.einsum(
        "qhe,khe->qhk", grad_heads, value_heads, preferred_element_type=jnp.float32
    )
    new_max = jnp.maximum(running_max, jnp.max(scores, axis=2))
    exponent = jnp.exp(scores - new_max[:, :, None])
    factor = jnp.exp(running_max - new_max)
    return (
        new_max,
        running_sum * factor + jnp.sum(exponent, axis=2),
        weighted * factor + jnp.sum(exponent * prob_grad, axis=2),
    )


def key_terms(
    query_heads,
    grad_heads,
    query_times,
    log_total,
    delta_rows,
    key_heads,
    value_heads,
    key_times,
    key_scale,
    value_scale,
):
    scores = masked_scores(query_heads, key_heads, query_times, key_times)
    probability = jnp.exp(scores - log_total[:, :, None])
    prob_grad = jnp.einsum(
        "qhe,khe->qhk", grad_heads, value_heads, preferred_element_type=jnp.float32
    )
    score_grad = (probability * (prob_grad - delta_rows[:, :, None])).astype(jnp.bfloat16)
    value_grad = jnp.einsum(
        "qhk,qhe->khe",
        probability.astype(jnp.bfloat16),
        grad_heads,
        preferred_element_type=jnp.float32,
    )
    key_grad = jnp.einsum(
        "qhk,qhe->khe", score_grad, query_heads, preferred_element_type=jnp.float32
    ) * HEAD_DIM ** (-0.5)
    key_count = key_heads.shape[0]
    return (
        key_grad.reshape(key_count, -1) * key_scale
        + jnp.roll(value_grad, HEADS // 2, axis=1).reshape(key_count, -1) * value_scale
    )


def on_device(
    stored_acts, queries, patch_times, key_gain, value_gain, conv_weight, prior_grad, loss_grad
):
    own_acts = stored_acts[0]
    own_queries = queries[0]
    own_times = patch_times[0].astype(jnp.float32)
    time_wire = patch_times[0].astype(jnp.bfloat16)
    key_scale = key_gain[0]
    value_scale = value_gain[0]
    row_count = own_acts.shape[0]
    feature_count = own_acts.shape[1]
    arrived = shifted(prior_grad[0], "pipe", -1)
    is_last = lax.axis_index("pipe") == lax.axis_size("pipe") - 1
    incoming = jnp.where(is_last, loss_grad, arrived)
    extended = padded_2(incoming, (("ctx", 0),), GY * GZ)
    conv_part = conv_backward(extended, conv_weight[0], row_count)
    query_heads = split_heads(own_queries)
    grad_heads = split_heads(incoming)
    start_stats = (
        jnp.full((row_count, HEADS), -1e30, jnp.float32),
        jnp.zeros((row_count, HEADS), jnp.float32),
        jnp.zeros((row_count, HEADS), jnp.float32),
    )

    def sweep_keys(running, segment):
        key_heads, value_heads = keys_values(segment[0], key_scale, value_scale)
        return (
            running_stats(
                running,
                query_heads,
                grad_heads,
                own_times,
                key_heads,
                value_heads,
                segment[1].astype(jnp.float32),
            ),
            None,
        )

    shard_part = (
        lax.all_gather(own_acts, "ctx", axis=0, tiled=True),
        lax.all_gather(time_wire, "ctx", axis=0, tiled=True),
    )
    running = start_stats
    segment_x = shard_part[0]
    length = segment_x.shape[0]
    block_size = math.gcd(length, 512)
    running, _ = lax.scan(
        sweep_keys,
        running,
        (
            segment_x.reshape(length // block_size, block_size, feature_count),
            shard_part[1].reshape(length // block_size, block_size),
        ),
    )
    running_max, running_sum, weighted = running
    log_total = running_max + jnp.log(running_sum)
    delta_rows = weighted / running_sum
    all_total, all_delta, all_times = (
        lax.all_gather(log_total, "ctx", axis=0, tiled=True),
        lax.all_gather(delta_rows, "ctx", axis=0, tiled=True),
        lax.all_gather(own_times, "ctx", axis=0, tiled=True),
    )
    own_keys, own_values = keys_values(own_acts, key_scale, value_scale)

    def sweep_queries(accumulated, segment):
        segment_q, segment_g, segment_times, segment_total, segment_delta = segment
        return (
            accumulated
            + key_terms(
                split_heads(segment_q),
                split_heads(segment_g),
                segment_times,
                segment_total,
                segment_delta,
                own_keys,
                own_values,
                own_times,
                key_scale,
                value_scale,
            ),
            None,
        )

    accumulated = jnp.zeros((row_count, feature_count), jnp.float32)
    shard_part = (
        lax.all_gather(own_queries, "ctx", axis=0, tiled=True),
        lax.all_gather(incoming, "ctx", axis=0, tiled=True),
    )
    length = shard_part[0].shape[0]
    block_size = math.gcd(length, 512)
    block_count = length // block_size
    segments = (
        shard_part[0].reshape(block_count, block_size, feature_count),
        shard_part[1].reshape(block_count, block_size, feature_count),
        all_times.reshape(block_count, block_size),
        all_total.reshape(block_count, block_size, HEADS),
        all_delta.reshape(block_count, block_size, HEADS),
    )
    accumulated, _ = lax.scan(sweep_queries, accumulated, segments)
    return (conv_part + accumulated).astype(jnp.bfloat16)[None]


def solution(mesh):
    in_specs = (
        P("pipe", "ctx", None),
        P("pipe", "ctx", None),
        P("pipe", "ctx"),
        P("pipe", None),
        P("pipe", None),
        P("pipe", None, None, None),
        P("pipe", "ctx", None),
        P("ctx", None),
    )
    out_specs = P("pipe", "ctx", None)
    return jax.shard_map(
        on_device, mesh=mesh, in_specs=in_specs, out_specs=out_specs, check_vma=False
    )
```

profile of v0, /device:TPU:1, one launch (start us, length us, event | category | flops | bytes accessed | tf_op | source)
XLA Modules:
  0.0 412.6 jit_solution(16347624726571813158)
XLA Ops:
  10.9 7.0 %collective-permute-done = bf16[128,1024]{0,1:T(8,128)(2,1)S(1)} collective-permute-done((bf16[128,1024]{0,1:T(8,128)(2,1)S(1)}, bf16[128,1024]{0,1:T(8,128)(2,1)S(1)}, u32[]{:S(2)}, u32[]{:S(2)}) %collective-permute-start) | collective-permute-done | bytes 262176 | tf_op jit(solution)/shard_map/ppermute | solution.py:20
  27.7 7.0 %collective-permute-start.1 = (bf16[64,1024]{0,1:T(8,128)(2,1)S(1)}, bf16[64,1024]{0,1:T(8,128)(2,1)S(1)}, u32[]{:S(2)}, u32[]{:S(2)}) collective-permute-start(bf16[64,1024]{0,1:T(8,128)(2,1)S(1)} %get-tuple-element.327), channel_id=1, source_target_pairs={{0,1},{1,2},{2,3},{3,4},{4,5},{5,6},{6,7},{7,8},{8,9},{9,10},{10,1... | collective-permute-start | bytes 393224 | tf_op jit(solution)/shard_map/ppermute | solution.py:28
  36.6 38.4 %all-gather.2 = bf16[1,4096]{1,0:T(2,128)(2,1)S(1)} all-gather(bf16[1,128]{1,0:T(2,128)(2,1)S(1)} %get-tuple-element.331), channel_id=4, replica_groups=mesh['pipe'=8,'ctx'=32] {'ctx'}, dimensions={1}, use_global_device_ids=true | all-gather | bytes 8448 | tf_op jit(solution)/shard_map/all_gather | solution.py:166
  75.0 31.7 %all-gather.1 = f32[1,4096]{1,0:T(1,128)S(1)} all-gather(f32[1,128]{1,0:T(1,128)S(1)} %get-tuple-element.333), channel_id=3, replica_groups=mesh['pipe'=8,'ctx'=32] {'ctx'}, dimensions={1}, use_global_device_ids=true | all-gather | bytes 16896 | tf_op jit(solution)/shard_map/all_gather | solution.py:186
  118.6 65.3 %while.26 = (s32[]{:T(128)}, f32[128,16]{0,1:T(8,128)S(1)}, f32[128,16]{0,1:T(8,128)S(1)}, f32[128,16]{0,1:T(8,128)S(1)}, bf16[8,512]{1,0:T(8,128)(2,1)S(1)}, /*...) while((s32[]{:T(128)}, f32[128,16]{0,1:T(8,128)S(1)}, ...), condition=%wide.region_4.5_spmd.clone, body=%wide.region_0.4_spmd.clone.sunk | while | flops 284768768 | bytes 24049328 | solution.py:172
  183.8 32.1 %all_gather.27 = f32[4096,16]{0,1:T(8,128)S(1)} all-gather(f32[128,16]{0,1:T(8,128)S(1)} %get-tuple-element.329), channel_id=1, replica_groups=mesh['pipe'=8,'ctx'=32] {'ctx'}, dimensions={0}, use_global_device_ids=true | all-gather | bytes 270336 | tf_op jit(solution)/shard_map/all_gather | solution.py:185
  216.8 32.9 %all_gather.25 = f32[4096,16]{0,1:T(8,128)S(1)} all-gather(f32[128,16]{0,1:T(8,128)S(1)} %get-tuple-element.330), channel_id=1, replica_groups=mesh['pipe'=8,'ctx'=32] {'ctx'}, dimensions={0}, use_global_device_ids=true | all-gather | bytes 270336 | tf_op jit(solution)/shard_map/all_gather | solution.py:184
  250.6 12.0 %copy.80 = bf16[4096,1024]{1,0:T(8,128)(2,1)} copy(bf16[4096,1024]{0,1:T(8,128)(2,1)} %all-gather.8.cloned.1.call-done) | data formatting | bytes 16777216 | tf_op jit(solution)/shard_map/all_gather | solution.py:212
  262.6 140.5 %while.27 = (s32[]{:T(128)}, f32[128,1024]{0,1:T(8,128)}, bf16[8,512,1024]{2,1,0:T(8,128)(2,1)}, f32[128]{0:T(128)S(1)}, f32[8,512]{1,0:T(8,128)}, /*index=5*/bf...) while((s32[]{:T(128)}, f32[128,1024]{0,1:T(8,128)}, ...), condition=%wide.region_6.7_spmd.clone, body=%wide.region_5.6_spmd.clone.sunk | while | flops 548339712 | bytes 35699416 | solution.py:224
  270.1 5.4 %fusion.142 = f32[16,64,128]{2,1,0:T(8,128)S(1)} fusion(bf16[512,16,64]{0,2,1:T(8,128)(2,1)S(1)} %bitcast.339, f32[16,512,128]{2,1,0:T(8,128)} %fusion.141, bf16[512,16,64]{0,2,1:T(8,128)(2,1)S(1)} %bitcast.340, bf16[128,16,64]{0,2,1:T(8,128)(2,1)} %get-tuple-element.576, f32[512,16]{0,1:T(8,128)S(1)} %bitcast.359, f32[512,16]{0,1:T(8,128)S(1)} %bitcast.357, ...), kind=kOutput, calls=%fused_computation.13.clone.1 | convolution fusion | flops 274857984 | bytes 7208960 | tf_op jit(solution)/shard_map/while/body/eval_jaxpr/qhk,qhe->khe/dot_general | solution.py:115
  275.5 3.2 fusion.143
  285.0 2.8 fusion.141
  287.7 5.4 %fusion.142 = f32[16,64,128]{2,1,0:T(8,128)S(1)} fusion(bf16[512,16,64]{0,2,1:T(8,128)(2,1)S(1)} %bitcast.339, f32[16,512,128]{2,1,0:T(8,128)} %fusion.141, bf16[512,16,64]{0,2,1:T(8,128)(2,1)S(1)} %bitcast.340, bf16[128,16,64]{0,2,1:T(8,128)(2,1)} %get-tuple-element.576, f32[512,16]{0,1:T(8,128)S(1)} %bitcast.359, f32[512,16]{0,1:T(8,128)S(1)} %bitcast.357, ...), kind=kOutput, calls=%fused_computation.13.clone.1 | convolution fusion | flops 274857984 | bytes 7208960 | tf_op jit(solution)/shard_map/while/body/eval_jaxpr/qhk,qhe->khe/dot_general | solution.py:115
  293.1 3.2 fusion.143
  302.5 2.8 fusion.141
  305.3 5.4 %fusion.142 = f32[16,64,128]{2,1,0:T(8,128)S(1)} fusion(bf16[512,16,64]{0,2,1:T(8,128)(2,1)S(1)} %bitcast.339, f32[16,512,128]{2,1,0:T(8,128)} %fusion.141, bf16[512,16,64]{0,2,1:T(8,128)(2,1)S(1)} %bitcast.340, bf16[128,16,64]{0,2,1:T(8,128)(2,1)} %get-tuple-element.576, f32[512,16]{0,1:T(8,128)S(1)} %bitcast.359, f32[512,16]{0,1:T(8,128)S(1)} %bitcast.357, ...), kind=kOutput, calls=%fused_computation.13.clone.1 | convolution fusion | flops 274857984 | bytes 7208960 | tf_op jit(solution)/shard_map/while/body/eval_jaxpr/qhk,qhe->khe/dot_general | solution.py:115
  310.6 3.2 fusion.143
  320.1 2.8 fusion.141
  322.8 5.4 %fusion.142 = f32[16,64,128]{2,1,0:T(8,128)S(1)} fusion(bf16[512,16,64]{0,2,1:T(8,128)(2,1)S(1)} %bitcast.339, f32[16,512,128]{2,1,0:T(8,128)} %fusion.141, bf16[512,16,64]{0,2,1:T(8,128)(2,1)S(1)} %bitcast.340, bf16[128,16,64]{0,2,1:T(8,128)(2,1)} %get-tuple-element.576, f32[512,16]{0,1:T(8,128)S(1)} %bitcast.359, f32[512,16]{0,1:T(8,128)S(1)} %bitcast.357, ...), kind=kOutput, calls=%fused_computation.13.clone.1 | convolution fusion | flops 274857984 | bytes 7208960 | tf_op jit(solution)/shard_map/while/body/eval_jaxpr/qhk,qhe->khe/dot_general | solution.py:115
  328.2 3.2 fusion.143
  337.6 2.8 fusion.141
  340.4 5.4 %fusion.142 = f32[16,64,128]{2,1,0:T(8,128)S(1)} fusion(bf16[512,16,64]{0,2,1:T(8,128)(2,1)S(1)} %bitcast.339, f32[16,512,128]{2,1,0:T(8,128)} %fusion.141, bf16[512,16,64]{0,2,1:T(8,128)(2,1)S(1)} %bitcast.340, bf16[128,16,64]{0,2,1:T(8,128)(2,1)} %get-tuple-element.576, f32[512,16]{0,1:T(8,128)S(1)} %bitcast.359, f32[512,16]{0,1:T(8,128)S(1)} %bitcast.357, ...), kind=kOutput, calls=%fused_computation.13.clone.1 | convolution fusion | flops 274857984 | bytes 7208960 | tf_op jit(solution)/shard_map/while/body/eval_jaxpr/qhk,qhe->khe/dot_general | solution.py:115
  345.8 3.2 fusion.143
  355.2 2.8 fusion.141
  358.0 5.4 %fusion.142 = f32[16,64,128]{2,1,0:T(8,128)S(1)} fusion(bf16[512,16,64]{0,2,1:T(8,128)(2,1)S(1)} %bitcast.339, f32[16,512,128]{2,1,0:T(8,128)} %fusion.141, bf16[512,16,64]{0,2,1:T(8,128)(2,1)S(1)} %bitcast.340, bf16[128,16,64]{0,2,1:T(8,128)(2,1)} %get-tuple-element.576, f32[512,16]{0,1:T(8,128)S(1)} %bitcast.359, f32[512,16]{0,1:T(8,128)S(1)} %bitcast.357, ...), kind=kOutput, calls=%fused_computation.13.clone.1 | convolution fusion | flops 274857984 | bytes 7208960 | tf_op jit(solution)/shard_map/while/body/eval_jaxpr/qhk,qhe->khe/dot_general | solution.py:115
  363.3 3.2 fusion.143
  372.8 2.8 fusion.141
  375.5 5.4 %fusion.142 = f32[16,64,128]{2,1,0:T(8,128)S(1)} fusion(bf16[512,16,64]{0,2,1:T(8,128)(2,1)S(1)} %bitcast.339, f32[16,512,128]{2,1,0:T(8,128)} %fusion.141, bf16[512,16,64]{0,2,1:T(8,128)(2,1)S(1)} %bitcast.340, bf16[128,16,64]{0,2,1:T(8,128)(2,1)} %get-tuple-element.576, f32[512,16]{0,1:T(8,128)S(1)} %bitcast.359, f32[512,16]{0,1:T(8,128)S(1)} %bitcast.357, ...), kind=kOutput, calls=%fused_computation.13.clone.1 | convolution fusion | flops 274857984 | bytes 7208960 | tf_op jit(solution)/shard_map/while/body/eval_jaxpr/qhk,qhe->khe/dot_general | solution.py:115
  380.9 3.2 fusion.143
  390.3 2.8 fusion.141
  393.1 5.4 %fusion.142 = f32[16,64,128]{2,1,0:T(8,128)S(1)} fusion(bf16[512,16,64]{0,2,1:T(8,128)(2,1)S(1)} %bitcast.339, f32[16,512,128]{2,1,0:T(8,128)} %fusion.141, bf16[512,16,64]{0,2,1:T(8,128)(2,1)S(1)} %bitcast.340, bf16[128,16,64]{0,2,1:T(8,128)(2,1)} %get-tuple-element.576, f32[512,16]{0,1:T(8,128)S(1)} %bitcast.359, f32[512,16]{0,1:T(8,128)S(1)} %bitcast.357, ...), kind=kOutput, calls=%fused_computation.13.clone.1 | convolution fusion | flops 274857984 | bytes 7208960 | tf_op jit(solution)/shard_map/while/body/eval_jaxpr/qhk,qhe->khe/dot_general | solution.py:115
  398.4 3.2 fusion.143
  (348 shorter events, 148.6 us)
Async XLA Ops:
  6.5 112.0 %all-gather.12.cloned.1.call-start = ((), (), s32[]{:S(2)}) async-start(), calls=%async_computation.2 | async-start | bytes 8650752 | tf_op jit(solution)/shard_map/all_gather | solution.py:165
  7.3 243.3 %all-gather.8.cloned.1.call-start = ((), (), s32[]{:S(2)}) async-start(), calls=%async_computation | async-start | bytes 8650752 | tf_op jit(solution)/shard_map/all_gather | solution.py:212
  8.4 9.4 %collective-permute-start = (bf16[128,1024]{0,1:T(8,128)(2,1)S(1)}, bf16[128,1024]{0,1:T(8,128)(2,1)S(1)}, u32[]{:S(2)}, u32[]{:S(2)}) collective-permute-start(bf16[128,1024]{0,1:T(8,128)(2,1)S(1)} %bitcast.363), channel_id=1, source_target_pairs={{32,0},{64,32},{96,64},{128,96},{160,128},{192,160},{224,192},{33,... | collective-permute-start | bytes 786440 | tf_op jit(solution)/shard_map/ppermute | solution.py:20
  18.6 93.5 %copy-start.2 = (bf16[128,1024]{0,1:T(8,128)(2,1)S(1)}, bf16[128,1024]{0,1:T(8,128)(2,1)}, u32[]{:S(2)}) copy-start(bf16[128,1024]{0,1:T(8,128)(2,1)} %broadcast_select_fusion) | copy-start | bytes 786436
  18.6 244.0 %all-gather.10.cloned.1.call-start = ((), (), s32[]{:S(2)}) async-start(), calls=%async_computation.1 | async-start | bytes 8650752 | tf_op jit(solution)/shard_map/all_gather | solution.py:211
  27.7 84.4 %collective-permute-start.1 = (bf16[64,1024]{0,1:T(8,128)(2,1)S(1)}, bf16[64,1024]{0,1:T(8,128)(2,1)S(1)}, u32[]{:S(2)}, u32[]{:S(2)}) collective-permute-start(bf16[64,1024]{0,1:T(8,128)(2,1)S(1)} %get-tuple-element.327), channel_id=1, source_target_pairs={{0,1},{1,2},{2,3},{3,4},{4,5},{5,6},{6,7},{7,8},{8,9},{9,10},{10,1... | collective-permute-start | bytes 393224 | tf_op jit(solution)/shard_map/ppermute | solution.py:28
  34.7 77.4 %collective-permute-start.2 = (bf16[64,1024]{0,1:T(8,128)(2,1)S(1)}, bf16[64,1024]{0,1:T(8,128)(2,1)S(1)}, u32[]{:S(2)}, u32[]{:S(2)}) collective-permute-start(bf16[64,1024]{0,1:T(8,128)(2,1)S(1)} %get-tuple-element.328), channel_id=1, source_target_pairs={{1,0},{2,1},{3,2},{4,3},{5,4},{6,5},{7,6},{8,7},{9,8},{10,9},{11,1... | collective-permute-start | bytes 393224 | tf_op jit(solution)/shard_map/ppermute | solution.py:31
  114.1 1.5 copy-start.3
  115.3 3.3 copy-start.4
  115.3 3.3 copy-start.5
  115.3 3.3 copy-start.6
  270.1 8.7 %copy-start = (f32[128,1024]{0,1:T(8,128)S(1)}, f32[128,1024]{0,1:T(8,128)}, u32[]{:S(2)}) copy-start(f32[128,1024]{0,1:T(8,128)} %get-tuple-element.555) | copy-start | bytes 1572868 | tf_op jit(solution)/shard_map/while
  279.3 0.8 copy-start.1
  287.7 8.7 %copy-start = (f32[128,1024]{0,1:T(8,128)S(1)}, f32[128,1024]{0,1:T(8,128)}, u32[]{:S(2)}) copy-start(f32[128,1024]{0,1:T(8,128)} %get-tuple-element.555) | copy-start | bytes 1572868 | tf_op jit(solution)/shard_map/while
  296.9 0.8 copy-start.1
  305.3 8.7 %copy-start = (f32[128,1024]{0,1:T(8,128)S(1)}, f32[128,1024]{0,1:T(8,128)}, u32[]{:S(2)}) copy-start(f32[128,1024]{0,1:T(8,128)} %get-tuple-element.555) | copy-start | bytes 1572868 | tf_op jit(solution)/shard_map/while
  314.5 0.8 copy-start.1
  322.8 8.7 %copy-start = (f32[128,1024]{0,1:T(8,128)S(1)}, f32[128,1024]{0,1:T(8,128)}, u32[]{:S(2)}) copy-start(f32[128,1024]{0,1:T(8,128)} %get-tuple-element.555) | copy-start | bytes 1572868 | tf_op jit(solution)/shard_map/while
  332.0 0.8 copy-start.1
  340.4 8.7 %copy-start = (f32[128,1024]{0,1:T(8,128)S(1)}, f32[128,1024]{0,1:T(8,128)}, u32[]{:S(2)}) copy-start(f32[128,1024]{0,1:T(8,128)} %get-tuple-element.555) | copy-start | bytes 1572868 | tf_op jit(solution)/shard_map/while
  349.6 0.8 copy-start.1
  358.0 8.7 %copy-start = (f32[128,1024]{0,1:T(8,128)S(1)}, f32[128,1024]{0,1:T(8,128)}, u32[]{:S(2)}) copy-start(f32[128,1024]{0,1:T(8,128)} %get-tuple-element.555) | copy-start | bytes 1572868 | tf_op jit(solution)/shard_map/while
  367.2 0.8 copy-start.1
  375.5 8.7 %copy-start = (f32[128,1024]{0,1:T(8,128)S(1)}, f32[128,1024]{0,1:T(8,128)}, u32[]{:S(2)}) copy-start(f32[128,1024]{0,1:T(8,128)} %get-tuple-element.555) | copy-start | bytes 1572868 | tf_op jit(solution)/shard_map/while
  384.7 0.8 copy-start.1
  393.1 8.7 %copy-start = (f32[128,1024]{0,1:T(8,128)S(1)}, f32[128,1024]{0,1:T(8,128)}, u32[]{:S(2)}) copy-start(f32[128,1024]{0,1:T(8,128)} %get-tuple-element.555) | copy-start | bytes 1572868 | tf_op jit(solution)/shard_map/while
  402.3 0.8 copy-start.1
Sparse Core Ops, SparseCore 0:
  9.2 77.7 all-gather.11
  88.8 88.8 all-gather.7
  179.6 71.0 all-gather.9
where the time goes:
time: 415 us; the launch traced here: 413 us
  blocking collectives  135 us (33%)
  matrix products  114 us (27%)
  local copies, waits for them, and re-layouts  94.5 us (23%)
  other arithmetic  34.7 us (8%)
  between operations  13.6 us (3%)
  starting transfers between devices  10.3 us (2%)
  waiting for transfers between devices  8.39 us (2%)
    dot_general x8, matrix products, key_terms(): jnp.einsum('qhk,qhe->khe', score_grad, query_heads, preferred_element_typ...  42.9 us
    all_gather x1, blocking collectives, on_device(): lax.all_gather(time_wire, 'ctx', axis=0, tiled=True)  38.4 us
    dynamic_slice x40, local copies, waits for them, and re-layouts, on_device(): lax.scan(sweep_keys, running, (segment_x.reshape(length // block_size, bl...  37.4 us
    all_gather x1, blocking collectives, on_device(): lax.all_gather(log_total, 'ctx', axis=0, tiled=True)  32.9 us
    all_gather x1, blocking collectives, on_device(): lax.all_gather(delta_rows, 'ctx', axis=0, tiled=True)  32.1 us
    all_gather x1, blocking collectives, on_device(): lax.all_gather(own_times, 'ctx', axis=0, tiled=True)  31.7 us
    dot_general x16, matrix products, masked_scores(): jnp.einsum('qhe,khe->qhk', query_heads, key_heads, preferred_element_type...  31.2 us
    dot_general x8, matrix products, key_terms(): jnp.einsum('qhk,qhe->khe', probability.astype(jnp.bfloat16), grad_heads,...  25.7 us
  transfers between devices with their start and end apart: 6, of which 1 were waited for; matrix products, arithmetic and copies ran while one was open for 24% of the time, Pallas kernels for 0%

commit v1 on v0

v1 whole, which is shorter than its diff:
```python
import functools

import jax
import jax.numpy as jnp
from jax import lax
from jax.experimental import pallas as pl
from jax.experimental.pallas import tpu as pltpu
from jax.sharding import Mesh, PartitionSpec as P

HEADS = 16
HEAD_DIM = 64
CHANNELS = 128
GY = 8
GZ = 8
D = 1024
FIELDS = 8
ROWS = 128
PAIR = 128
RING = 8
TIMES = 32
CHUNK = 16
QPOS = 32
HIDDEN = -1e30
ALL = ("pipe", "y", "z", "core")
BF16 = jnp.bfloat16
F32 = jnp.float32


def column(row):
    return jnp.transpose(jnp.broadcast_to(row, (ROWS, ROWS)))


def order_matrix(times_row):
    across = jnp.broadcast_to(times_row, (ROWS, ROWS))
    down = jnp.transpose(across)
    i = lax.broadcasted_iota(jnp.int32, (ROWS, ROWS), 0)
    j = lax.broadcasted_iota(jnp.int32, (ROWS, ROWS), 1)
    before = jnp.where((down < across) | ((down == across) & (i < j)), 1.0, 0.0)
    rank = jnp.sum(before, axis=0, keepdims=True)
    return jnp.where(i.astype(F32) == rank, 1.0, 0.0)


def pair_columns(rows, pair, swap):
    low = rows[:, pair * HEAD_DIM : (pair + 1) * HEAD_DIM]
    high = rows[:, D // 2 + pair * HEAD_DIM : D // 2 + (pair + 1) * HEAD_DIM]
    return jnp.concatenate([high, low] if swap else [low, high], axis=1)


def pack_acts_kernel(times_ref, acts_ref, queries_ref, acts_out, queries_out):
    order = order_matrix(times_ref[0:1, :])
    low_order = order.astype(BF16)
    times = jnp.sum(order * column(times_ref[0:1, :]).T, axis=1, keepdims=True)
    times_row = jnp.transpose(jnp.broadcast_to(times, (ROWS, ROWS)))[0:16, :].astype(BF16)
    for source, target in ((acts_ref, acts_out), (queries_ref, queries_out)):
        ordered = jnp.dot(low_order, source[...], preferred_element_type=F32)
        for pair in range(RING):
            target[pair, 0:ROWS, :] = pair_columns(ordered, pair, False).astype(BF16)
    for pair in range(RING):
        acts_out[pair, ROWS : ROWS + 16, :] = times_row


def pack_grad_kernel(times_ref, grad_ref, grad_out):
    low_order = order_matrix(times_ref[0:1, :]).astype(BF16)
    ordered = jnp.dot(low_order, grad_ref[...], preferred_element_type=F32)
    for pair in range(RING):
        grad_out[pair] = pair_columns(ordered, pair, True).astype(BF16)


def unpack_kernel(times_ref, parts_ref, conv_ref, out_ref):
    low_order = order_matrix(times_ref[0:1, :]).astype(BF16)
    for pair in range(0, RING, 2):
        spans = []
        for one in (pair, pair + 1):
            spans.append(
                lax.dot_general(
                    low_order, parts_ref[one], (((0,), (0,)), ((), ())), preferred_element_type=F32
                )
            )
        low = jnp.concatenate([spans[0][:, :HEAD_DIM], spans[1][:, :HEAD_DIM]], axis=1)
        high = jnp.concatenate([spans[0][:, HEAD_DIM:], spans[1][:, HEAD_DIM:]], axis=1)
        at = pair * HEAD_DIM
        for start, block in ((at, low), (D // 2 + at, high)):
            span = slice(start, start + 2 * HEAD_DIM)
            out_ref[:, span] = (conv_ref[:, span] + block).astype(BF16)


def attention_kernel(
    acts_a, acts_b, acts_c, acts_d, queries_ref, grads_ref, gains_ref,
    near_ref, far_ref,
    keys, values, biases, scores, exps, key_acc, value_acc,
):
    key_gain = gains_ref[0:1, :]
    value_gain = gains_ref[1:2, :]
    lane = lax.broadcasted_iota(jnp.int32, (ROWS, PAIR), 1)
    lane_times = lane.astype(F32)
    key_acc[...] = jnp.zeros_like(key_acc)
    value_acc[...] = jnp.zeros_like(value_acc)
    firsts = None
    for group, acts in enumerate((acts_a, acts_b, acts_c, acts_d)):
        for source in range(RING):
            block = group * RING + source
            rows = acts[source, 0:ROWS, :].astype(F32)
            times_row = acts[source, ROWS : ROWS + 16, :].astype(F32)[0:1, :]
            firsts = times_row if firsts is None else jnp.minimum(firsts, times_row)
            times = column(times_row)
            keys[block, :, 0:PAIR] = (rows * key_gain).astype(BF16)
            keys[block, :, PAIR : 2 * PAIR] = jnp.where(lane_times == times, 1.0, 0.0).astype(BF16)
            values[block] = (rows * value_gain).astype(BF16)
            if group == 0:
                biases[source] = jnp.where(lane_times > times, HIDDEN, 0.0).astype(BF16)
                lasts = times_row if source == 0 else jnp.maximum(lasts, times_row)

    blocks = 4 * RING
    height = blocks * CHUNK
    width = RING * QPOS
    pos = lax.broadcasted_iota(jnp.int32, (1, ROWS), 1)
    upper = lax.broadcasted_iota(jnp.int32, (width, PAIR), 1) >= HEAD_DIM

    for q in range(ROWS // QPOS):
        latest = jnp.max(jnp.where(pos == (q + 1) * QPOS - 1, lasts, -1.0))
        starts = (firsts <= latest) & (pos % CHUNK == 0)
        visible = jnp.sum(jnp.where(starts, 1, 0))
        at = q * QPOS
        q_rows = queries_ref[:, at : at + QPOS, :].reshape(width, PAIR)
        g_rows = grads_ref[:, at : at + QPOS, :].reshape(width, PAIR)
        bias = biases[:, at : at + QPOS, :].reshape(width, PAIR)
        q_rows = q_rows.astype(F32) * HEAD_DIM**-0.5
        g_rows = g_rows.astype(F32)
        for head in range(2):
            own = upper if head else ~upper
            other = ~upper if head else upper
            q_head = jnp.where(own, q_rows, 0.0)
            g_head = jnp.where(other, g_rows, 0.0)
            q_low = jnp.concatenate([q_head.astype(BF16), bias], axis=1)
            g_low = g_head.astype(BF16)

            def find_max(c, top):
                rows = keys[:, pl.ds(pl.multiple_of(c * CHUNK, CHUNK), CHUNK), :].reshape(height, 2 * PAIR)
                s = lax.dot_general(rows, q_low, (((1,), (1,)), ((), ())), preferred_element_type=F32)
                scores[c] = s
                return jnp.maximum(top, jnp.max(s.reshape(height // 8, 8, width), axis=0))

            top = lax.fori_loop(0, visible, find_max, jnp.full((8, width), -jnp.inf, F32))
            top = jnp.max(top, axis=0, keepdims=True)

            def find_sums(c, sums):
                total, weighted = sums
                rows = values[:, pl.ds(pl.multiple_of(c * CHUNK, CHUNK), CHUNK), :].reshape(height, PAIR)
                dp = lax.dot_general(rows, g_low, (((1,), (1,)), ((), ())), preferred_element_type=F32)
                e = jnp.exp(scores[c] - top)
                exps[c] = e.astype(BF16)
                scores[c] = dp
                total = total + jnp.sum(e.reshape(height // 8, 8, width), axis=0)
                weighted = weighted + jnp.sum((e * dp).reshape(height // 8, 8, width), axis=0)
                return total, weighted

            zero = jnp.zeros((8, width), F32)
            total, weighted = lax.fori_loop(0, visible, find_sums, (zero, zero))
            inverse = 1.0 / jnp.sum(total, axis=0, keepdims=True)
            delta = jnp.sum(weighted, axis=0, keepdims=True) * inverse
            scale = jnp.concatenate(
                [column(inverse[:, k * ROWS : (k + 1) * ROWS]) for k in range(width // ROWS)], axis=0
            )
            q_scaled = (q_head * scale).astype(BF16)
            g_scaled = (g_head * scale).astype(BF16)

            def add_up(c, carry):
                span = pl.ds(pl.multiple_of(c * CHUNK, CHUNK), CHUNK)
                e = exps[c]
                ds = (e.astype(F32) * (scores[c] - delta)).astype(BF16)
                dv = jnp.dot(e, g_scaled, preferred_element_type=F32)
                dk = jnp.dot(ds, q_scaled, preferred_element_type=F32)
                value_acc[:, span, :] += dv.reshape(blocks, CHUNK, PAIR)
                key_acc[:, span, :] += dk.reshape(blocks, CHUNK, PAIR)
                return carry

            lax.fori_loop(0, visible, add_up, 0)

    for block in range(blocks):
        out = (key_acc[block] * key_gain + value_acc[block] * value_gain).astype(BF16)
        if block < 2 * RING:
            near_ref[block] = out
        else:
            far_ref[block - 2 * RING] = out


def in_vmem(count):
    return [pl.BlockSpec(memory_space=pltpu.VMEM)] * count


def pack_acts(times_row, acts, queries):
    return pl.pallas_call(
        pack_acts_kernel,
        out_shape=(
            jax.ShapeDtypeStruct((RING, ROWS + 16, PAIR), BF16),
            jax.ShapeDtypeStruct((RING, ROWS, PAIR), BF16),
        ),
        in_specs=in_vmem(3),
        out_specs=tuple(in_vmem(2)),
        cost_estimate=pl.CostEstimate(flops=2 * ROWS * ROWS * 2 * D, bytes_accessed=8 * ROWS * D, transcendentals=0),
    )(times_row, acts, queries)


def pack_grad(times_row, grad):
    return pl.pallas_call(
        pack_grad_kernel,
        out_shape=jax.ShapeDtypeStruct((RING, ROWS, PAIR), BF16),
        in_specs=in_vmem(2),
        out_specs=in_vmem(1)[0],
        cost_estimate=pl.CostEstimate(flops=2 * ROWS * ROWS * D, bytes_accessed=4 * ROWS * D, transcendentals=0),
    )(times_row, grad)


def unpack(times_row, parts, conv):
    return pl.pallas_call(
        unpack_kernel,
        out_shape=jax.ShapeDtypeStruct((ROWS, D), BF16),
        in_specs=in_vmem(3),
        out_specs=in_vmem(1)[0],
        cost_estimate=pl.CostEstimate(flops=2 * ROWS * ROWS * D, bytes_accessed=8 * ROWS * D, transcendentals=0),
    )(times_row, parts, conv)


def attention(acts, queries, grads, gains):
    chunks = ROWS // CHUNK
    height = 4 * RING * CHUNK
    width = RING * QPOS
    tokens = 4 * RING * ROWS
    return pl.pallas_call(
        attention_kernel,
        out_shape=(jax.ShapeDtypeStruct((2 * RING, ROWS, PAIR), BF16),) * 2,
        in_specs=in_vmem(7),
        out_specs=tuple(in_vmem(2)),
        scratch_shapes=[
            pltpu.VMEM((4 * RING, ROWS, 2 * PAIR), BF16),
            pltpu.VMEM((4 * RING, ROWS, PAIR), BF16),
            pltpu.VMEM((RING, ROWS, PAIR), BF16),
            pltpu.VMEM((chunks, height, width), F32),
            pltpu.VMEM((chunks, height, width), BF16),
            pltpu.VMEM((4 * RING, ROWS, PAIR), F32),
            pltpu.VMEM((4 * RING, ROWS, PAIR), F32),
        ],
        compiler_params=pltpu.CompilerParams(vmem_limit_bytes=40 * 1024 * 1024),
        cost_estimate=pl.CostEstimate(
            flops=2 * 4 * 2 * RING * ROWS * tokens * PAIR, bytes_accessed=4 * tokens * PAIR, transcendentals=2 * RING * ROWS * tokens
        ),
    )(*acts, queries, grads, gains)


def conv_backward(extended, weight, row_count):
    planes = row_count // (GY * GZ)
    grid_field = extended.reshape(planes + 2, GY, GZ, FIELDS, CHANNELS)
    padded = jnp.pad(grid_field, ((0, 0), (1, 1), (1, 1), (0, 0), (0, 0)))
    windows = []
    for shift_x in (-1, 0, 1):
        for shift_y in (-1, 0, 1):
            for shift_z in (-1, 0, 1):
                windows.append(
                    padded[
                        1 - shift_x : 1 - shift_x + planes,
                        1 - shift_y : 1 - shift_y + GY,
                        1 - shift_z : 1 - shift_z + GZ,
                    ]
                )
    stacked = jnp.stack(windows, axis=4).reshape(row_count * FIELDS, 27 * CHANNELS)
    matrix = jnp.transpose(weight, (0, 2, 1)).reshape(27 * CHANNELS, CHANNELS)
    return jnp.dot(stacked, matrix, preferred_element_type=F32).reshape(row_count, D)


def swapped(value, axis):
    return lax.ppermute(value, axis, [(0, 1), (1, 0)])


def exchanged(value):
    return lax.all_to_all(value, "z", split_axis=0, concat_axis=0, tiled=True)


def pair_gains(gain, pair):
    low = lax.dynamic_slice_in_dim(gain, pair * HEAD_DIM, HEAD_DIM, 1)
    high = lax.dynamic_slice_in_dim(gain, D // 2 + pair * HEAD_DIM, HEAD_DIM, 1)
    return jnp.concatenate([low, high], axis=1)


def on_device(
    sections, blocks, stored_acts, queries, patch_times, key_gain, value_gain, conv_weight, prior_grad, loss_grad
):
    times_row = patch_times.astype(F32)
    section = lax.axis_index("pipe")
    pair = lax.axis_index("z")
    sent = jnp.where(section == 0, loss_grad, prior_grad[0])
    edge = GY * GZ

    def from_next(value, step):
        perm = []
        for s in range(sections):
            for b in range(blocks):
                if 0 <= b + step < blocks:
                    perm.append((s * blocks + b, (s - 1) % sections * blocks + b + step))
        return lax.ppermute(value, ALL, perm)

    incoming = from_next(sent, 0)
    low = from_next(sent[ROWS - edge :], 1)
    high = from_next(sent[:edge], -1)

    acts_out, queries_out = pack_acts(times_row, stored_acts[0], queries[0])
    own = exchanged(acts_out)
    query_rows = exchanged(queries_out)
    grad_rows = exchanged(pack_grad(times_row, incoming))
    across = swapped(own, "y")
    own_core = swapped(own, "core")
    across_core = swapped(across, "core")

    extended = jnp.concatenate([low, incoming, high], axis=0)
    conv_part = conv_backward(extended, conv_weight[0], ROWS)

    gains = jnp.concatenate([pair_gains(key_gain, pair), pair_gains(value_gain, pair), jnp.zeros((6, PAIR), F32)], axis=0)
    near, far = attention((own, across, own_core, across_core), query_rows, grad_rows, gains)
    near = near.astype(F32) + swapped(far, "core").astype(F32)
    mine = near[:RING] + swapped(near[RING:].astype(BF16), "y").astype(F32)
    parts = exchanged(mine.astype(BF16))
    return unpack(times_row, parts, conv_part)[None]


def solution(mesh):
    sections, blocks = mesh.devices.shape
    fine = Mesh(mesh.devices.reshape(sections, 2, RING, 2), ALL)
    ctx = ("y", "z", "core")
    in_specs = (
        P("pipe", ctx, None),
        P("pipe", ctx, None),
        P("pipe", ctx),
        P("pipe", None),
        P("pipe", None),
        P("pipe", None, None, None),
        P("pipe", ctx, None),
        P(ctx, None),
    )
    return jax.shard_map(
        functools.partial(on_device, sections, blocks),
        mesh=fine,
        in_specs=in_specs,
        out_specs=P("pipe", ctx, None),
        check_vma=False,
    )
```

time: 415 us -> 153 us (0.37)
  blocking collectives: 135 us -> 0 us
  matrix products: 114 us -> 4.99 us
  local copies, waits for them, and re-layouts: 94.5 us -> 25.4 us
  Pallas kernels: 0 us -> 52.3 us
  starting transfers between devices: 10.3 us -> 50.4 us
  other arithmetic: 34.7 us -> 3.34 us
  between operations: 13.6 us -> 0.16 us
  waiting for transfers between devices: 8.39 us -> 16.1 us
    all_gather x4 -> x0, blocking collectives: 135 us -> none  [the longest x1 38.4 us: on_device(): lax.all_gather(time_wire, 'ctx', axis=0, tiled=True)]
    dot_general x41 -> x1, matrix products: 114 us -> 4.99 us  [conv_backward(): jnp.dot(stacked, matrix, preferred_element_type=F32).reshape(row_count, D)]
    pallas_call x0 -> x4, Pallas kernels: none -> 52.3 us  [the longest x1 45.7 us: attention(): pl.pallas_call(attention_kernel, out_shape=(jax.ShapeDtypeStruct((2 * RIN...]
    dynamic_slice x72 -> x1, local copies, waits for them, and re-layouts: 52 us -> 0.78 us  [pair_gains(): low = lax.dynamic_slice_in_dim(gain, pair * HEAD_DIM, HEAD_DIM, 1)]
    all_to_all x0 -> x4, starting transfers between devices: none -> 21.7 us  [exchanged(): return lax.all_to_all(value, 'z', split_axis=0, concat_axis=0, tiled=True)]
    ppermute x3 -> x8, starting transfers between devices: 10.2 us -> 28.7 us  [the longest x5 15.5 us: swapped(): return lax.ppermute(value, axis, [(0, 1), (1, 0)])]
    all_gather x2 -> x0, local copies, waits for them, and re-layouts: 12.5 us -> none  [the longest x1 12 us: on_device(): lax.all_gather(incoming, 'ctx', axis=0, tiled=True)]
    while x49 -> x0, local copies, waits for them, and re-layouts: 12.2 us -> none
  transfers between devices with their start and end apart: 6 -> 12, of which waited for: 1 -> 4; matrix products, arithmetic and copies ran while one was open for 24% -> 20% of each run, Pallas kernels for 0% -> 3%
where the time goes in v1:
time: 153 us
  Pallas kernels  52.3 us (34%)
  starting transfers between devices  50.4 us (33%)
  local copies, waits for them, and re-layouts  25.4 us (17%)
  waiting for transfers between devices  16.1 us (11%)
  matrix products  4.99 us (3%)
  other arithmetic  3.34 us (2%)
    pallas_call x1, Pallas kernels, attention(): pl.pallas_call(attention_kernel, out_shape=(jax.ShapeDtypeStruct((2 * RIN...  45.7 us
    unnamed x31, local copies, waits for them, and re-layouts  22.7 us
    all_to_all x4, starting transfers between devices, exchanged(): return lax.all_to_all(value, 'z', split_axis=0, concat_axis=0, tiled=True)  21.7 us
    ppermute x5, starting transfers between devices, swapped(): return lax.ppermute(value, axis, [(0, 1), (1, 0)])  15.5 us
    ppermute x3, starting transfers between devices, from_next(): return lax.ppermute(value, ALL, perm)  13.3 us
    all_to_all x4, waiting for transfers between devices, exchanged(): return lax.all_to_all(value, 'z', split_axis=0, concat_axis=0, tiled=True)  11.7 us
    dot_general x1, matrix products, conv_backward(): jnp.dot(stacked, matrix, preferred_element_type=F32).reshape(row_count, D)  4.99 us
    ppermute x5, waiting for transfers between devices, swapped(): return lax.ppermute(value, axis, [(0, 1), (1, 0)])  4.38 us
  transfers between devices with their start and end apart: 12, of which 4 were waited for; matrix products, arithmetic and copies ran while one was open for 20% of the time, Pallas kernels for 3%

profile of v1, /device:TPU:1, one launch (start us, length us, event | category | flops | bytes accessed | tf_op | source)
XLA Modules:
  0.0 152.6 jit_solution(120173593484239359)
XLA Ops:
  0.0 1.1 bitcast_select_fusion
  1.1 5.9 %collective-permute-start.3 = (bf16[128,1024]{1,0:T(8,128)(2,1)S(1)}, bf16[128,1024]{1,0:T(8,128)(2,1)S(1)}, u32[]{:S(2)}, u32[]{:S(2)}) collective-permute-start(bf16[128,1024]{1,0:T(8,128)(2,1)S(1)} %bitcast_select_fusion), channel_id=1, source_target_pairs={{0,224},{1,225},{2,226},{3,227},{4,228},{5,229},{6,230},{7,231},{8... | collective-permute-start | bytes 786440 | tf_op jit(solution)/shard_map/ppermute | solution.py:299
  7.0 4.2 %collective-permute-start.6 = (bf16[64,1024]{1,0:T(8,128)(2,1)S(1)}, bf16[64,1024]{1,0:T(8,128)(2,1)S(1)}, u32[]{:S(2)}, u32[]{:S(2)}) collective-permute-start(bf16[64,1024]{1,0:T(8,128)(2,1)S(1)} %get-tuple-element.15), channel_id=1, source_target_pairs={{0,225},{1,226},{2,227},{3,228},{4,229},{5,230},{6,231},{7,232},{8... | collective-permute-start | bytes 393224 | tf_op jit(solution)/shard_map/ppermute | solution.py:299
  11.2 3.2 %collective-permute-start.7 = (bf16[64,1024]{1,0:T(8,128)(2,1)S(1)}, bf16[64,1024]{1,0:T(8,128)(2,1)S(1)}, u32[]{:S(2)}, u32[]{:S(2)}) collective-permute-start(bf16[64,1024]{1,0:T(8,128)(2,1)S(1)} %get-tuple-element.16), channel_id=1, source_target_pairs={{1,224},{2,225},{3,226},{4,227},{5,228},{6,229},{7,230},{8,231},{9... | collective-permute-start | bytes 393224 | tf_op jit(solution)/shard_map/ppermute | solution.py:299
  14.4 1.2 convert_element_type.18.times_ref
  15.6 2.2 %shard_map.82 = (bf16[8,144,128]{2,1,0:T(8,128)(2,1)}, bf16[8,128,128]{2,1,0:T(8,128)(2,1)}) custom-call(f32[1,128]{1,0:T(1,128)} %convert_element_type.18.times_ref, bf16[128,1024]{1,0:T(8,128)(2,1)} %bitcast.164, bf16[128,1024]{1,0:T(8,128)(2,1)} %bitcast.165), custom_call_target="tpu_custom_call" | custom-call | flops 67108864 | bytes 1048576 | tf_op jit(solution)/shard_map/pallas_call | solution.py:192
  17.9 8.2 %all-to-all-start = ((bf16[8,144,128]{2,1,0:T(8,128)(2,1)}), bf16[8,144,128]{2,1,0:T(8,128)(2,1)S(1)}, u32[]{:S(2)}, u32[]{:S(2)}) async-start(bf16[8,144,128]{2,1,0:T(8,128)(2,1)} %get-tuple-element.9), calls=%async_computation | async-start | bytes 589824 | tf_op jit(solution)/shard_map/all_to_all | solution.py:275
  26.8 1.9 %copy.36 = bf16[1,27,128,128]{2,3,1,0:T(8,128)(2,1)S(1)} copy(bf16[1,27,128,128]{3,2,1,0:T(8,128)(2,1)} %param.13) | data formatting | bytes 1769472 | tf_op args[5]
  29.1 0.8 fusion.2
  29.9 0.8 fusion.4
  32.2 0.8 copy_dynamic-update-slice_fusion.2
  33.8 0.8 fusion.12
  36.1 0.8 fusion.18
  39.2 6.6 %all-to-all-start.1 = ((bf16[8,128,128]{2,1,0:T(8,128)(2,1)}), bf16[8,128,128]{2,1,0:T(8,128)(2,1)S(1)}, u32[]{:S(2)}, u32[]{:S(2)}) async-start(bf16[8,128,128]{2,1,0:T(8,128)(2,1)} %get-tuple-element.10), calls=%async_computation.1 | async-start | bytes 524288 | tf_op jit(solution)/shard_map/all_to_all | solution.py:275
  45.9 0.8 copy_dynamic-update-slice_fusion.1
  47.8 2.1 %shard_map.83 = bf16[8,128,128]{2,1,0:T(8,128)(2,1)} custom-call(f32[1,128]{1,0:T(1,128)} %convert_element_type.18.times_ref, bf16[128,1024]{1,0:T(8,128)(2,1)} %copy-done), custom_call_target="tpu_custom_call" | custom-call | flops 33554432 | bytes 524288 | tf_op jit(solution)/shard_map/pallas_call | solution.py:205
  50.7 4.7 %all-to-all-done.1.queries_ref = bf16[8,128,128]{2,1,0:T(8,128)(2,1)S(1)} async-done(((bf16[8,128,128]{2,1,0:T(8,128)(2,1)}), bf16[8,128,128]{2,1,0:T(8,128)(2,1)S(1)}, u32[]{:S(2)}, u32[]{:S(2)}) %all-to-all-start.1) | async-done | bytes 262176 | tf_op jit(solution)/shard_map/all_to_all | solution.py:275
  55.4 3.4 %all-to-all-start.2 = ((bf16[8,128,128]{2,1,0:T(8,128)(2,1)}), bf16[8,128,128]{2,1,0:T(8,128)(2,1)S(1)}, u32[]{:S(2)}, u32[]{:S(2)}) async-start(bf16[8,128,128]{2,1,0:T(8,128)(2,1)} %shard_map.83), calls=%async_computation.2 | async-start | bytes 524288 | tf_op jit(solution)/shard_map/all_to_all | solution.py:275
  59.5 4.9 %collective-permute-start.1 = (bf16[8,144,128]{2,1,0:T(8,128)(2,1)S(1)}, bf16[8,144,128]{2,1,0:T(8,128)(2,1)S(1)}, u32[]{:S(2)}, u32[]{:S(2)}) collective-permute-start(bf16[8,144,128]{2,1,0:T(8,128)(2,1)S(1)} %all-to-all-done.acts_a), channel_id=1, source_target_pairs={{0,1},{1,0},{2,3},{3,2},{4,5},{5,4},{6,7},{7,6},{8,9},{9,8},{10,11... | collective-permute-start | bytes 884744 | tf_op jit(solution)/shard_map/ppermute | solution.py:271
  65.2 0.8 fusion.34
  66.7 1.3 all-to-all-done.2.grads_ref
  68.0 45.7 %shard_map.84 = (bf16[16,128,128]{2,1,0:T(8,128)(2,1)S(1)}, bf16[16,128,128]{2,1,0:T(8,128)(2,1)S(1)}) custom-call(bf16[8,144,128]{2,1,0:T(8,128)(2,1)S(1)} %all-to-all-done.acts_a, bf16[8,144,128]{2,1,0:T(8,128)(2,1)S(1)} %collective-permute-done.acts_b, bf16[8,144,128]{2,1,0:T(8,128)(2,1)S(1)} %collective-permute-done.1.acts_c, ...), custom_call_target="tpu_custom_call" | custom-call | flops 8589934592 | bytes 2097152 | tf_op jit(solution)/shard_map/pallas_call | solution.py:229
  113.7 8.0 %collective-permute-start.4 = (bf16[16,128,128]{2,1,0:T(8,128)(2,1)S(1)}, bf16[16,128,128]{2,1,0:T(8,128)(2,1)S(1)}, u32[]{:S(2)}, u32[]{:S(2)}) collective-permute-start(bf16[16,128,128]{2,1,0:T(8,128)(2,1)S(1)} %get-tuple-element.12), channel_id=1, source_target_pairs={{0,1},{1,0},{2,3},{3,2},{4,5},{5,4},{6,7},{7,6},{8,9},{9,8},{10,11... | collective-permute-start | bytes 1572872 | tf_op jit(solution)/shard_map/ppermute | solution.py:271
  121.7 0.8 fusion.38
  124.0 0.8 fusion.42
  125.0 2.2 %collective-permute-start.5 = (bf16[8,128,128]{2,1,0:T(8,128)(2,1)S(1)}, bf16[8,128,128]{2,1,0:T(8,128)(2,1)S(1)}, u32[]{:S(2)}, u32[]{:S(2)}) collective-permute-start(bf16[8,128,128]{2,1,0:T(8,128)(2,1)S(1)} %slice.258), channel_id=1, source_target_pairs={{0,16},{16,0},{1,17},{17,1},{2,18},{18,2},{3,19},{19,3},{4,20},{20... | collective-permute-start | bytes 786440 | tf_op jit(solution)/shard_map/ppermute | solution.py:271
  129.4 4.4 %collective-permute-done.5 = bf16[8,128,128]{2,1,0:T(8,128)(2,1)S(1)} collective-permute-done((bf16[8,128,128]{2,1,0:T(8,128)(2,1)S(1)}, bf16[8,128,128]{2,1,0:T(8,128)(2,1)S(1)}, u32[]{:S(2)}, u32[]{:S(2)}) %collective-permute-start.5) | collective-permute-done | bytes 262176 | tf_op jit(solution)/shard_map/ppermute | solution.py:271
  134.6 3.4 %all-to-all-start.3 = ((bf16[8,128,128]{2,1,0:T(8,128)(2,1)}), bf16[8,128,128]{2,1,0:T(8,128)(2,1)S(1)}, u32[]{:S(2)}, u32[]{:S(2)}) async-start(bf16[8,128,128]{2,1,0:T(8,128)(2,1)} %fusion), calls=%async_computation.3 | async-start | bytes 524288 | tf_op jit(solution)/shard_map/all_to_all | solution.py:275
  138.0 5.0 %fusion.50 = f32[1024,128]{1,0:T(8,128)S(1)} fusion(bf16[1024,3456]{1,0:T(8,128)(2,1)} %bitcast.54, bf16[3456,128]{1,0:T(8,128)(2,1)S(1)} %bitcast.163), kind=kOutput, calls=%fused_computation.89 | convolution fusion | flops 905969664 | bytes 8486912 | tf_op jit(solution)/shard_map/dot_general | solution.py:267
  143.0 0.9 reshape.21.conv_ref
  143.9 5.7 %all-to-all-done.3.parts_ref = bf16[8,128,128]{2,1,0:T(8,128)(2,1)S(1)} async-done(((bf16[8,128,128]{2,1,0:T(8,128)(2,1)}), bf16[8,128,128]{2,1,0:T(8,128)(2,1)S(1)}, u32[]{:S(2)}, u32[]{:S(2)}) %all-to-all-start.3) | async-done | bytes 262176 | tf_op jit(solution)/shard_map/all_to_all | solution.py:275
  150.3 2.4 %shard_map.85 = bf16[128,1024]{1,0:T(8,128)(2,1)} custom-call(f32[1,128]{1,0:T(1,128)} %convert_element_type.18.times_ref, bf16[8,128,128]{2,1,0:T(8,128)(2,1)} %copy-done.1, f32[128,1024]{1,0:T(8,128)} %reshape.21.conv_ref), custom_call_target="tpu_custom_call" | custom-call | flops 33554432 | bytes 1048576 | tf_op jit(solution)/shard_map/pallas_call | solution.py:215
  (43 shorter events, 16.9 us)
Async XLA Ops:
  1.1 27.8 %collective-permute-start.3 = (bf16[128,1024]{1,0:T(8,128)(2,1)S(1)}, bf16[128,1024]{1,0:T(8,128)(2,1)S(1)}, u32[]{:S(2)}, u32[]{:S(2)}) collective-permute-start(bf16[128,1024]{1,0:T(8,128)(2,1)S(1)} %bitcast_select_fusion), channel_id=1, source_target_pairs={{0,224},{1,225},{2,226},{3,227},{4,228},{5,229},{6,230},{7,231},{8... | collective-permute-start | bytes 786440 | tf_op jit(solution)/shard_map/ppermute | solution.py:299
  7.0 21.9 %collective-permute-start.6 = (bf16[64,1024]{1,0:T(8,128)(2,1)S(1)}, bf16[64,1024]{1,0:T(8,128)(2,1)S(1)}, u32[]{:S(2)}, u32[]{:S(2)}) collective-permute-start(bf16[64,1024]{1,0:T(8,128)(2,1)S(1)} %get-tuple-element.15), channel_id=1, source_target_pairs={{0,225},{1,226},{2,227},{3,228},{4,229},{5,230},{6,231},{7,232},{8... | collective-permute-start | bytes 393224 | tf_op jit(solution)/shard_map/ppermute | solution.py:299
  11.2 17.7 %collective-permute-start.7 = (bf16[64,1024]{1,0:T(8,128)(2,1)S(1)}, bf16[64,1024]{1,0:T(8,128)(2,1)S(1)}, u32[]{:S(2)}, u32[]{:S(2)}) collective-permute-start(bf16[64,1024]{1,0:T(8,128)(2,1)S(1)} %get-tuple-element.16), channel_id=1, source_target_pairs={{1,224},{2,225},{3,226},{4,227},{5,228},{6,229},{7,230},{8,231},{9... | collective-permute-start | bytes 393224 | tf_op jit(solution)/shard_map/ppermute | solution.py:299
  17.9 21.4 %all-to-all-start = ((bf16[8,144,128]{2,1,0:T(8,128)(2,1)}), bf16[8,144,128]{2,1,0:T(8,128)(2,1)S(1)}, u32[]{:S(2)}, u32[]{:S(2)}) async-start(bf16[8,144,128]{2,1,0:T(8,128)(2,1)} %get-tuple-element.9), calls=%async_computation | async-start | bytes 589824 | tf_op jit(solution)/shard_map/all_to_all | solution.py:275
  28.9 17.8 %copy-start = (bf16[128,1024]{1,0:T(8,128)(2,1)}, bf16[128,1024]{1,0:T(8,128)(2,1)S(1)}, u32[]{:S(2)}) copy-start(bf16[128,1024]{1,0:T(8,128)(2,1)S(1)} %collective-permute-done.3.grad_ref) | copy-start | bytes 786436
  39.2 16.1 %all-to-all-start.1 = ((bf16[8,128,128]{2,1,0:T(8,128)(2,1)}), bf16[8,128,128]{2,1,0:T(8,128)(2,1)S(1)}, u32[]{:S(2)}, u32[]{:S(2)}) async-start(bf16[8,128,128]{2,1,0:T(8,128)(2,1)} %get-tuple-element.10), calls=%async_computation.1 | async-start | bytes 524288 | tf_op jit(solution)/shard_map/all_to_all | solution.py:275
  46.7 17.8 %collective-permute-start = (bf16[8,144,128]{2,1,0:T(8,128)(2,1)S(1)}, bf16[8,144,128]{2,1,0:T(8,128)(2,1)S(1)}, u32[]{:S(2)}, u32[]{:S(2)}) collective-permute-start(bf16[8,144,128]{2,1,0:T(8,128)(2,1)S(1)} %all-to-all-done.acts_a), channel_id=1, source_target_pairs={{0,16},{16,0},{1,17},{17,1},{2,18},{18,2},{3,19},{19,3},{4,20},{20... | collective-permute-start | bytes 884744 | tf_op jit(solution)/shard_map/ppermute | solution.py:271
  55.4 12.7 %all-to-all-start.2 = ((bf16[8,128,128]{2,1,0:T(8,128)(2,1)}), bf16[8,128,128]{2,1,0:T(8,128)(2,1)S(1)}, u32[]{:S(2)}, u32[]{:S(2)}) async-start(bf16[8,128,128]{2,1,0:T(8,128)(2,1)} %shard_map.83), calls=%async_computation.2 | async-start | bytes 524288 | tf_op jit(solution)/shard_map/all_to_all | solution.py:275
  59.5 8.5 %collective-permute-start.1 = (bf16[8,144,128]{2,1,0:T(8,128)(2,1)S(1)}, bf16[8,144,128]{2,1,0:T(8,128)(2,1)S(1)}, u32[]{:S(2)}, u32[]{:S(2)}) collective-permute-start(bf16[8,144,128]{2,1,0:T(8,128)(2,1)S(1)} %all-to-all-done.acts_a), channel_id=1, source_target_pairs={{0,1},{1,0},{2,3},{3,2},{4,5},{5,4},{6,7},{7,6},{8,9},{9,8},{10,11... | collective-permute-start | bytes 884744 | tf_op jit(solution)/shard_map/ppermute | solution.py:271
  64.4 3.6 %collective-permute-start.2 = (bf16[8,144,128]{2,1,0:T(8,128)(2,1)S(1)}, bf16[8,144,128]{2,1,0:T(8,128)(2,1)S(1)}, u32[]{:S(2)}, u32[]{:S(2)}) collective-permute-start(bf16[8,144,128]{2,1,0:T(8,128)(2,1)S(1)} %collective-permute-done.acts_b), channel_id=1, source_target_pairs={{0,1},{1,0},{2,3},{3,2},{4,5},{5,4},{6,7},{7,6},{8,9},{9,8},{10,11... | collective-permute-start | bytes 884744 | tf_op jit(solution)/shard_map/ppermute | solution.py:271
  113.7 11.1 %collective-permute-start.4 = (bf16[16,128,128]{2,1,0:T(8,128)(2,1)S(1)}, bf16[16,128,128]{2,1,0:T(8,128)(2,1)S(1)}, u32[]{:S(2)}, u32[]{:S(2)}) collective-permute-start(bf16[16,128,128]{2,1,0:T(8,128)(2,1)S(1)} %get-tuple-element.12), channel_id=1, source_target_pairs={{0,1},{1,0},{2,3},{3,2},{4,5},{5,4},{6,7},{7,6},{8,9},{9,8},{10,11... | collective-permute-start | bytes 1572872 | tf_op jit(solution)/shard_map/ppermute | solution.py:271
  125.0 8.8 %collective-permute-start.5 = (bf16[8,128,128]{2,1,0:T(8,128)(2,1)S(1)}, bf16[8,128,128]{2,1,0:T(8,128)(2,1)S(1)}, u32[]{:S(2)}, u32[]{:S(2)}) collective-permute-start(bf16[8,128,128]{2,1,0:T(8,128)(2,1)S(1)} %slice.258), channel_id=1, source_target_pairs={{0,16},{16,0},{1,17},{17,1},{2,18},{18,2},{3,19},{19,3},{4,20},{20... | collective-permute-start | bytes 786440 | tf_op jit(solution)/shard_map/ppermute | solution.py:271
  134.6 15.0 %all-to-all-start.3 = ((bf16[8,128,128]{2,1,0:T(8,128)(2,1)}), bf16[8,128,128]{2,1,0:T(8,128)(2,1)S(1)}, u32[]{:S(2)}, u32[]{:S(2)}) async-start(bf16[8,128,128]{2,1,0:T(8,128)(2,1)} %fusion), calls=%async_computation.3 | async-start | bytes 524288 | tf_op jit(solution)/shard_map/all_to_all | solution.py:275
  149.6 0.7 copy-start.1

commit v2 on v1

v2 whole, which is shorter than its diff:
```python
import functools

import jax
import jax.numpy as jnp
from jax import lax
from jax.experimental import pallas as pl
from jax.experimental.pallas import tpu as pltpu
from jax.sharding import Mesh, PartitionSpec as P

HEADS = 16
HEAD_DIM = 64
CHANNELS = 128
GY = 8
GZ = 8
D = 1024
FIELDS = 8
ROWS = 128
PAIR = 128
RING = 8
NOTES = 16
CHUNK = 32
QPOS = 32
HIDDEN = -1e30
ALL = ("pipe", "y", "z", "core")
BF16 = jnp.bfloat16
F32 = jnp.float32


def column(row):
    return jnp.transpose(jnp.broadcast_to(row, (ROWS, ROWS)))


def order_matrix(times_row):
    across = jnp.broadcast_to(times_row, (ROWS, ROWS))
    down = jnp.transpose(across)
    i = lax.broadcasted_iota(jnp.int32, (ROWS, ROWS), 0)
    j = lax.broadcasted_iota(jnp.int32, (ROWS, ROWS), 1)
    before = jnp.where((down < across) | ((down == across) & (i < j)), 1.0, 0.0)
    rank = jnp.sum(before, axis=0, keepdims=True)
    return jnp.where(i.astype(F32) == rank, 1.0, 0.0)


def pair_columns(rows, pair, swap):
    low = rows[:, pair * HEAD_DIM : (pair + 1) * HEAD_DIM]
    high = rows[:, D // 2 + pair * HEAD_DIM : D // 2 + (pair + 1) * HEAD_DIM]
    return jnp.concatenate([high, low] if swap else [low, high], axis=1)


def pack_kernel(place_ref, times_ref, acts_ref, queries_ref, prior_ref, loss_ref, rows_out):
    section = place_ref[1]
    times_row = times_ref[0:1, :].astype(F32)
    order = order_matrix(times_row)
    low_order = order.astype(BF16)
    sorted_times = jnp.sum(order * jnp.broadcast_to(times_row, (ROWS, ROWS)), axis=1, keepdims=True)
    sorted_row = jnp.transpose(jnp.broadcast_to(sorted_times, (ROWS, ROWS)))[0:8, :]
    notes = jnp.concatenate([sorted_row, jnp.broadcast_to(times_row, (8, ROWS))], axis=0).astype(BF16)
    for source, first in ((acts_ref, 0), (queries_ref, ROWS + NOTES)):
        ordered = jnp.dot(low_order, source[...], preferred_element_type=F32)
        for pair in range(RING):
            rows_out[pair, first : first + ROWS, :] = pair_columns(ordered, pair, False).astype(BF16)
    for pair in range(RING):
        rows_out[pair, ROWS : ROWS + NOTES, :] = notes
    sent = jnp.where(section == 0, loss_ref[...].astype(F32), prior_ref[...].astype(F32))
    for pair in range(RING):
        rows_out[pair, 2 * ROWS + NOTES :, :] = pair_columns(sent, pair, True).astype(BF16)


def unpack_kernel(times_ref, parts_ref, conv_ref, out_ref):
    low_order = order_matrix(times_ref[0:1, :].astype(F32)).astype(BF16)
    for pair in range(0, RING, 2):
        spans = []
        for one in (pair, pair + 1):
            halves = [
                lax.dot_general(
                    low_order, parts_ref[half * RING + one], (((0,), (0,)), ((), ())), preferred_element_type=F32
                )
                for half in range(2)
            ]
            spans.append(halves[0] + halves[1])
        low = jnp.concatenate([spans[0][:, :HEAD_DIM], spans[1][:, :HEAD_DIM]], axis=1)
        high = jnp.concatenate([spans[0][:, HEAD_DIM:], spans[1][:, HEAD_DIM:]], axis=1)
        at = pair * HEAD_DIM
        for start, block in ((at, low), (D // 2 + at, high)):
            span = slice(start, start + 2 * HEAD_DIM)
            out_ref[:, span] = (conv_ref[:, span] + block).astype(BF16)


def attention_kernel(
    place_ref, acts_a, acts_b, acts_c, acts_d, *rest
):
    grads_in, gains_ref, near_ref, far_ref = rest[:4]
    (
        grads, keys, values, biases, scores_a, scores_b, slopes_a, slopes_b, key_acc, value_acc,
    ) = rest[4:]
    lane_y = place_ref[2]
    key_gain = gains_ref[0:1, :]
    value_gain = gains_ref[1:2, :]
    lane = lax.broadcasted_iota(jnp.int32, (ROWS, PAIR), 1)
    lane_times = lane.astype(F32)
    key_acc[...] = jnp.zeros_like(key_acc)
    value_acc[...] = jnp.zeros_like(value_acc)
    firsts = None
    for group, acts in enumerate((acts_a, acts_b, acts_c, acts_d)):
        for source in range(RING):
            block = group * RING + source
            rows = acts[source, 0:ROWS, :].astype(F32)
            times_row = acts[source, ROWS : ROWS + NOTES, :].astype(F32)[0:1, :]
            firsts = times_row if firsts is None else jnp.minimum(firsts, times_row)
            times = column(times_row)
            keys[block, :, 0:PAIR] = (rows * key_gain).astype(BF16)
            keys[block, :, PAIR : 2 * PAIR] = jnp.where(lane_times == times, 1.0, 0.0).astype(BF16)
            values[block] = (rows * value_gain).astype(BF16)
            if group == 0:
                biases[source] = jnp.where(lane_times > times, HIDDEN, 0.0).astype(BF16)
                lasts = times_row if source == 0 else jnp.maximum(lasts, times_row)

    for source in range(RING):
        raw_row = acts_a[source, ROWS : ROWS + NOTES, :].astype(F32)[8:9, :]
        low_order = order_matrix(raw_row).astype(BF16)
        grads[source] = jnp.dot(low_order, grads_in[source], preferred_element_type=F32).astype(BF16)

    blocks = 4 * RING
    height = blocks * CHUNK
    width = RING * QPOS
    pos = lax.broadcasted_iota(jnp.int32, (1, ROWS), 1)
    upper = lax.broadcasted_iota(jnp.int32, (width, PAIR), 1) >= HEAD_DIM

    both = 2 * width
    nt = (((1,), (1,)), ((), ()))

    def folded(rows, combine):
        return combine(rows.reshape(height // 8, 8, both), axis=0)

    def first_pass(c, stats, q_low, g_low, scores, slopes):
        top, total, weighted = stats
        span = pl.ds(pl.multiple_of(c * CHUNK, CHUNK), CHUNK)
        s = lax.dot_general(keys[:, span, :].reshape(height, 2 * PAIR), q_low, nt, preferred_element_type=F32)
        scores[c] = s
        dp = lax.dot_general(values[:, span, :].reshape(height, PAIR), g_low, nt, preferred_element_type=F32)
        slopes[c] = dp
        new_top = jnp.maximum(top, jnp.max(folded(s, jnp.max), axis=0, keepdims=True))
        e = jnp.exp(s - new_top)
        factor = jnp.exp(top - new_top)
        return new_top, total * factor + folded(e, jnp.sum), weighted * factor + folded(e * dp, jnp.sum)

    def second_pass(c, shift, delta, q_low, g_low, scores, slopes):
        span = pl.ds(pl.multiple_of(c * CHUNK, CHUNK), CHUNK)
        p = jnp.exp(scores[c] - shift)
        ds = (p * (slopes[c] - delta)).astype(BF16)
        dv = jnp.dot(p.astype(BF16), g_low, preferred_element_type=F32)
        dk = jnp.dot(ds, q_low[:, :PAIR], preferred_element_type=F32)
        value_acc[:, span, :] += dv.reshape(blocks, CHUNK, PAIR)
        key_acc[:, span, :] += dk.reshape(blocks, CHUNK, PAIR)

    earlier = None
    seen = 0
    for q in range(ROWS // QPOS):
        latest = jnp.max(jnp.where(pos == (q + 1) * QPOS - 1, lasts, -1.0))
        starts = (firsts <= latest) & (pos % CHUNK == 0)
        visible = jnp.sum(jnp.where(starts, 1, 0))
        at = q * QPOS
        q_rows = acts_a[:, ROWS + NOTES + at : ROWS + NOTES + at + QPOS, :].reshape(width, PAIR).astype(F32) * HEAD_DIM**-0.5
        g_rows = grads[:, at : at + QPOS, :].reshape(width, PAIR).astype(F32)
        bias = biases[:, at : at + QPOS, :].reshape(width, PAIR)
        q_both = jnp.concatenate([jnp.where(upper, 0.0, q_rows), jnp.where(upper, q_rows, 0.0)], axis=0)
        g_both = jnp.concatenate([jnp.where(upper, g_rows, 0.0), jnp.where(upper, 0.0, g_rows)], axis=0)
        q_low = jnp.concatenate([q_both.astype(BF16), jnp.concatenate([bias, bias], axis=0)], axis=1)
        g_low = g_both.astype(BF16)
        buffers = (scores_a, slopes_a) if q % 2 == 0 else (scores_b, slopes_b)

        def merged(c, stats):
            second_pass(c, *earlier)
            return first_pass(c, stats, q_low, g_low, *buffers)

        def alone(c, stats):
            return first_pass(c, stats, q_low, g_low, *buffers)

        zero = jnp.zeros((8, both), F32)
        stats = (jnp.full((1, both), -1e30, F32), zero, zero)
        if earlier is not None:
            stats = lax.fori_loop(0, seen, merged, stats)
        stats = lax.fori_loop(seen, visible, alone, stats)
        top, total, weighted = stats
        total = jnp.sum(total, axis=0, keepdims=True)
        delta = jnp.sum(weighted, axis=0, keepdims=True) / total
        earlier = (top + jnp.log(total), delta, q_low, g_low, *buffers)
        seen = visible

    def last(c, carry):
        second_pass(c, *earlier)
        return carry

    lax.fori_loop(0, seen, last, 0)

    for block in range(blocks):
        out = (key_acc[block] * key_gain + value_acc[block] * value_gain).astype(BF16)
        side = block // RING % 2
        target = near_ref if block < 2 * RING else far_ref
        target[(lane_y if side == 0 else 1 - lane_y) * RING + block % RING] = out


def in_vmem(count):
    return [pl.BlockSpec(memory_space=pltpu.VMEM)] * count


def pack(place, times, acts, queries, prior, loss):
    smem = pl.BlockSpec(memory_space=pltpu.SMEM)
    return pl.pallas_call(
        pack_kernel,
        out_shape=jax.ShapeDtypeStruct((RING, 3 * ROWS + NOTES, PAIR), BF16),
        in_specs=[smem, *in_vmem(5)],
        out_specs=in_vmem(1)[0],
        cost_estimate=pl.CostEstimate(flops=2 * ROWS * ROWS * 2 * D, bytes_accessed=14 * ROWS * D, transcendentals=0),
    )(place, times, acts, queries, prior, loss)


def unpack(times_row, parts, conv):
    return pl.pallas_call(
        unpack_kernel,
        out_shape=jax.ShapeDtypeStruct((ROWS, D), BF16),
        in_specs=in_vmem(3),
        out_specs=in_vmem(1)[0],
        cost_estimate=pl.CostEstimate(flops=2 * ROWS * ROWS * D, bytes_accessed=8 * ROWS * D, transcendentals=0),
    )(times_row, parts, conv)


def attention(place, acts, grads, gains):
    chunks = ROWS // CHUNK
    height = 4 * RING * CHUNK
    width = RING * QPOS
    tokens = 4 * RING * ROWS
    return pl.pallas_call(
        attention_kernel,
        out_shape=(jax.ShapeDtypeStruct((2 * RING, ROWS, PAIR), BF16),) * 2,
        in_specs=[pl.BlockSpec(memory_space=pltpu.SMEM), *in_vmem(6)],
        out_specs=tuple(in_vmem(2)),
        scratch_shapes=[
            pltpu.VMEM((RING, ROWS, PAIR), BF16),
            pltpu.VMEM((4 * RING, ROWS, 2 * PAIR), BF16),
            pltpu.VMEM((4 * RING, ROWS, PAIR), BF16),
            pltpu.VMEM((RING, ROWS, PAIR), BF16),
            pltpu.VMEM((chunks, height, 2 * width), F32),
            pltpu.VMEM((chunks, height, 2 * width), F32),
            pltpu.VMEM((chunks, height, 2 * width), F32),
            pltpu.VMEM((chunks, height, 2 * width), F32),
            pltpu.VMEM((4 * RING, ROWS, PAIR), F32),
            pltpu.VMEM((4 * RING, ROWS, PAIR), F32),
        ],
        compiler_params=pltpu.CompilerParams(vmem_limit_bytes=56 * 1024 * 1024),
        cost_estimate=pl.CostEstimate(
            flops=2 * 4 * 2 * RING * ROWS * tokens * PAIR, bytes_accessed=4 * tokens * PAIR, transcendentals=2 * RING * ROWS * tokens
        ),
    )(place, *acts, grads, gains)


def conv_kernel(low_ref, rows_ref, high_ref, weight_ref, out_ref, padded):
    edge = GY * GZ
    planes = ROWS // edge + 2
    z = lax.broadcasted_iota(jnp.int32, (edge, CHANNELS), 0) % GZ
    empty = jnp.zeros((planes, GZ, 3 * CHANNELS), F32)
    for field in range(FIELDS):
        span = slice(field * CHANNELS, (field + 1) * CHANNELS)
        padded[field, :, 0] = empty
        padded[field, :, GY + 1] = empty
        for plane in range(planes):
            if plane == 0:
                rows = low_ref[:, span]
            elif plane == planes - 1:
                rows = high_ref[:, span]
            else:
                rows = rows_ref[(plane - 1) * edge : plane * edge, span]
            rows = rows.astype(F32)
            after = jnp.where(z == GZ - 1, 0.0, jnp.concatenate([rows[1:], rows[:1]], axis=0))
            before = jnp.where(z == 0, 0.0, jnp.concatenate([rows[-1:], rows[:-1]], axis=0))
            wide = jnp.concatenate([after, rows, before], axis=1)
            padded[field, plane, 1 : GY + 1] = wide.reshape(GY, GZ, 3 * CHANNELS)
    total = None
    for shift_x in (-1, 0, 1):
        for shift_y in (-1, 0, 1):
            first = 9 * (shift_x + 1) + 3 * (shift_y + 1)
            matrix = jnp.concatenate([weight_ref[first + k] for k in range(3)], axis=1)
            window = padded[:, 1 - shift_x : planes - 1 - shift_x, 1 - shift_y : 1 - shift_y + GY]
            part = lax.dot_general(
                window.astype(BF16).reshape(FIELDS * ROWS, 3 * CHANNELS),
                matrix,
                (((1,), (1,)), ((), ())),
                preferred_element_type=F32,
            )
            total = part if total is None else total + part
    for field in range(FIELDS):
        out_ref[:, field * CHANNELS : (field + 1) * CHANNELS] = total[field * ROWS : (field + 1) * ROWS]


def conv_backward(low, rows, high, weight):
    planes = ROWS // (GY * GZ) + 2
    return pl.pallas_call(
        conv_kernel,
        out_shape=jax.ShapeDtypeStruct((ROWS, D), F32),
        in_specs=in_vmem(4),
        out_specs=in_vmem(1)[0],
        scratch_shapes=[pltpu.VMEM((FIELDS, planes, GY + 2, GZ, 3 * CHANNELS), F32)],
        compiler_params=pltpu.CompilerParams(vmem_limit_bytes=24 * 1024 * 1024),
        cost_estimate=pl.CostEstimate(flops=2 * 27 * ROWS * D * CHANNELS, bytes_accessed=8 * ROWS * D, transcendentals=0),
    )(low, rows, high, weight)


def swapped(value, axis):
    return lax.ppermute(value, axis, [(0, 1), (1, 0)])


def exchanged(value, axis):
    return lax.all_to_all(value, axis, split_axis=0, concat_axis=0, tiled=True)


def pair_gains(gain, pair):
    low = lax.dynamic_slice_in_dim(gain, pair * HEAD_DIM, HEAD_DIM, 1)
    high = lax.dynamic_slice_in_dim(gain, D // 2 + pair * HEAD_DIM, HEAD_DIM, 1)
    return jnp.concatenate([low, high], axis=1)


def on_device(
    sections, blocks, stored_acts, queries, patch_times, key_gain, value_gain, conv_weight, prior_grad, loss_grad
):
    section, side, ring = lax.axis_index("pipe"), lax.axis_index("y"), lax.axis_index("z")
    place = jnp.stack([ring, section, side]).astype(jnp.int32)

    def from_next(value, step):
        perm = []
        for s in range(sections):
            for b in range(blocks):
                if 0 <= b + step < blocks:
                    perm.append((s * blocks + b, (s - 1) % sections * blocks + b + step))
        return lax.ppermute(value, ALL, perm)

    rows_out = pack(place, patch_times, stored_acts[0], queries[0], prior_grad[0], loss_grad)
    own = exchanged(rows_out, "z")
    grads = from_next(own[:, 2 * ROWS + NOTES :], 0)
    own_acts = own[:, : ROWS + NOTES]
    across = swapped(own_acts, "y")
    own_core = swapped(own_acts, "core")
    across_core = swapped(across, "core")

    gains = jnp.concatenate([pair_gains(key_gain, ring), pair_gains(value_gain, ring), jnp.zeros((6, PAIR), F32)], axis=0)
    near, far = attention(place, (own, across, own_core, across_core), grads, gains)

    near, edges = lax.optimization_barrier((near, jnp.where(section == 0, loss_grad, prior_grad[0])))
    incoming = from_next(edges, 0)
    low = from_next(edges[ROWS - GY * GZ :], 1)
    high = from_next(edges[: GY * GZ], -1)
    conv_part = conv_backward(low, incoming, high, conv_weight[0])

    mine = (near.astype(F32) + swapped(far, "core").astype(F32)).astype(BF16)
    parts = exchanged(mine, ("y", "z"))
    return unpack(patch_times, parts, conv_part)[None]


def solution(mesh):
    sections, blocks = mesh.devices.shape
    fine = Mesh(mesh.devices.reshape(sections, 2, RING, 2), ALL)
    ctx = ("y", "z", "core")
    in_specs = (
        P("pipe", ctx, None),
        P("pipe", ctx, None),
        P("pipe", ctx),
        P("pipe", None),
        P("pipe", None),
        P("pipe", None, None, None),
        P("pipe", ctx, None),
        P(ctx, None),
    )
    return jax.shard_map(
        functools.partial(on_device, sections, blocks),
        mesh=fine,
        in_specs=in_specs,
        out_specs=P("pipe", ctx, None),
        check_vma=False,
    )
```

time: 153 us -> 113 us (0.74); the launches traced: 153 us -> 111 us
  blocking collectives: 0 us -> 31.1 us
  starting transfers between devices: 50.4 us -> 25.5 us
  local copies, waits for them, and re-layouts: 25.4 us -> 4 us
  Pallas kernels: 52.3 us -> 34.4 us
  matrix products: 4.99 us -> 0 us
  waiting for transfers between devices: 16.1 us -> 13.7 us
    all_to_all x0 -> x1, blocking collectives: none -> 31.1 us  [exchanged(): return lax.all_to_all(value, axis, split_axis=0, concat_axis=0, tiled=True)]
    unnamed x31 -> x22, local copies, waits for them, and re-layouts: 22.7 us -> 3.09 us
    pallas_call x1, Pallas kernels: 45.7 us -> 27.3 us  [attention(): pl.pallas_call(attention_kernel, out_shape=(jax.ShapeDtypeStruct((2 * RIN...]
    all_to_all x4 -> x1, starting transfers between devices: 21.7 us -> 3.7 us  [exchanged(): return lax.all_to_all(value, axis, split_axis=0, concat_axis=0, tiled=True)]
    ppermute x3 -> x4, waiting for transfers between devices: 0.01 us -> 12 us  [from_next(): return lax.ppermute(value, ALL, perm)]
    all_to_all x4 -> x1, waiting for transfers between devices: 11.7 us -> 0.01 us  [exchanged(): return lax.all_to_all(value, axis, split_axis=0, concat_axis=0, tiled=True)]
    ppermute x5 -> x4, starting transfers between devices: 15.5 us -> 7.2 us  [swapped(): return lax.ppermute(value, axis, [(0, 1), (1, 0)])]
    dot_general x1 -> x0, matrix products: 4.99 us -> none  [conv_backward(): jnp.dot(stacked, matrix, preferred_element_type=F32).reshape(row_count, D)]
  transfers between devices with their start and end apart: 12 -> 9, of which waited for: 4 -> 3; matrix products, arithmetic and copies ran while one was open for 20% -> 1% of each run, Pallas kernels for 3% -> 2%
where the time goes in v2:
time: 113 us; the launch traced here: 111 us
  Pallas kernels  34.4 us (30%)
  blocking collectives  31.1 us (28%)
  starting transfers between devices  25.5 us (23%)
  waiting for transfers between devices  13.7 us (12%)
  local copies, waits for them, and re-layouts  4 us (4%)
  other arithmetic  2.31 us (2%)
    all_to_all x1, blocking collectives, exchanged(): return lax.all_to_all(value, axis, split_axis=0, concat_axis=0, tiled=True)  31.1 us
    pallas_call x1, Pallas kernels, attention(): pl.pallas_call(attention_kernel, out_shape=(jax.ShapeDtypeStruct((2 * RIN...  27.3 us
    ppermute x4, starting transfers between devices, from_next(): return lax.ppermute(value, ALL, perm)  14.6 us
    ppermute x4, waiting for transfers between devices, from_next(): return lax.ppermute(value, ALL, perm)  12 us
    ppermute x4, starting transfers between devices, swapped(): return lax.ppermute(value, axis, [(0, 1), (1, 0)])  7.2 us
    all_to_all x1, starting transfers between devices, exchanged(): return lax.all_to_all(value, axis, split_axis=0, concat_axis=0, tiled=True)  3.7 us
    unnamed x22, local copies, waits for them, and re-layouts  3.09 us
    pallas_call x1, Pallas kernels, pack(): pl.pallas_call(pack_kernel, out_shape=jax.ShapeDtypeStruct((RING, 3 * ROW...  2.6 us
  transfers between devices with their start and end apart: 9, of which 3 were waited for; matrix products, arithmetic and copies ran while one was open for 1% of the time, Pallas kernels for 2%

profile of v2, /device:TPU:1, one launch (start us, length us, event | category | flops | bytes accessed | tf_op | source)
XLA Modules:
  0.0 111.1 jit_solution(8550082811876397156)
XLA Ops:
  0.0 0.7 pad_add_fusion.place_ref
  0.7 2.6 %shard_map.82 = bf16[8,400,128]{2,1,0:T(8,128)(2,1)} custom-call(s32[3]{0:T(128)} %pad_add_fusion.place_ref, s32[1,128]{1,0:T(1,128)} %times_ref.3, bf16[128,1024]{1,0:T(8,128)(2,1)} %bitcast.11, bf16[128,1024]{1,0:T(8,128)(2,1)} %bitcast.12, bf16[128,1024]{1,0:T(8,128)(2,1)} %bitcast.10, bf16[128,1024]{1,0:T(8,128)(2,1)} %loss_ref.1), custom_call_target="tpu_custom_call" | custom-call | flops 67108864 | bytes 1835008 | tf_op jit(solution)/shard_map/pallas_call | solution.py:208
  3.3 31.1 %all_to_all.10.acts_a = bf16[8,400,128]{2,1,0:T(8,128)(2,1)S(1)} all-to-all(bf16[8,400,128]{2,1,0:T(8,128)(2,1)} %shard_map.82), channel_id=1, replica_groups=mesh['pipe'=8,'y'=2,'z'=8,'core'=2] {'z'}, dimensions={0} | all-to-all | bytes 1638400 | tf_op jit(solution)/shard_map/all_to_all | solution.py:312
  34.4 1.4 %collective-permute-start = (bf16[8,144,128]{2,1,0:T(8,128)(2,1)S(1)}, bf16[8,144,128]{2,1,0:T(8,128)(2,1)S(1)}, u32[]{:S(2)}, u32[]{:S(2)}) collective-permute-start(bf16[8,144,128]{2,1,0:T(8,128)(2,1)S(1)} %slice.16), channel_id=1, source_target_pairs={{0,16},{16,0},{1,17},{17,1},{2,18},{18,2},{3,19},{19,3},{4,20},{20... | collective-permute-start | bytes 884744 | tf_op jit(solution)/shard_map/ppermute | solution.py:308
  35.8 3.0 %collective-permute-start.1 = (bf16[8,144,128]{2,1,0:T(8,128)(2,1)S(1)}, bf16[8,144,128]{2,1,0:T(8,128)(2,1)S(1)}, u32[]{:S(2)}, u32[]{:S(2)}) collective-permute-start(bf16[8,144,128]{2,1,0:T(8,128)(2,1)S(1)} %slice.16), channel_id=1, source_target_pairs={{0,1},{1,0},{2,3},{3,2},{4,5},{5,4},{6,7},{7,6},{8,9},{9,8},{10,11... | collective-permute-start | bytes 884744 | tf_op jit(solution)/shard_map/ppermute | solution.py:308
  38.8 4.9 %collective-permute-start.3 = (bf16[8,128,128]{2,1,0:T(8,128)(2,1)S(1)}, bf16[8,128,128]{2,1,0:T(8,128)(2,1)S(1)}, u32[]{:S(2)}, u32[]{:S(2)}) collective-permute-start(bf16[8,128,128]{2,1,0:T(8,128)(2,1)S(1)} %slice.17), channel_id=1, source_target_pairs={{0,224},{1,225},{2,226},{3,227},{4,228},{5,229},{6,230},{7,231},{8... | collective-permute-start | bytes 786440 | tf_op jit(solution)/shard_map/ppermute | solution.py:333
  43.6 0.0 collective-permute-done.acts_b
  43.6 0.3 collective-permute-start.2
  43.9 0.8 constant_dynamic-slice_fusion.1
  44.7 0.1 pad.4.clone
  44.8 0.7 maximum_maximum_fusion.rest_1_
  45.5 3.9 %collective-permute-done.3.rest_0_ = bf16[8,128,128]{2,1,0:T(8,128)(2,1)S(1)} collective-permute-done((bf16[8,128,128]{2,1,0:T(8,128)(2,1)S(1)}, bf16[8,128,128]{2,1,0:T(8,128)(2,1)S(1)}, u32[]{:S(2)}, u32[]{:S(2)}) %collective-permute-start.3) | collective-permute-done | bytes 262176 | tf_op jit(solution)/shard_map/ppermute | solution.py:333
  49.4 0.0 collective-permute-done.1.acts_c
  49.4 0.0 collective-permute-done.2.acts_d
  49.4 0.7 copy-done.10
  50.1 0.1 copy-done.8
  50.2 0.7 copy-done.9
  50.9 27.3 %shard_map.83 = (bf16[16,128,128]{2,1,0:T(8,128)(2,1)}, bf16[16,128,128]{2,1,0:T(8,128)(2,1)}) custom-call(s32[3]{0:T(128)} %pad_add_fusion.place_ref, bf16[8,400,128]{2,1,0:T(8,128)(2,1)} %copy-done.2, bf16[8,144,128]{2,1,0:T(8,128)(2,1)} %copy-done.7, bf16[8,144,128]{2,1,0:T(8,128)(2,1)} %copy-done.8, bf16[8,144,128]{2,1,0:T(8,128)(2,1)} %copy-done.9, ...), custom_call_target="tpu_custom_call" | custom-call | flops 8589934592 | bytes 2097152 | tf_op jit(solution)/shard_map/pallas_call | solution.py:232
  78.2 2.6 %collective-permute-start.4 = (bf16[16,128,128]{2,1,0:T(8,128)(2,1)}, bf16[16,128,128]{2,1,0:T(8,128)(2,1)S(1)}, u32[]{:S(2)}, u32[]{:S(2)}) collective-permute-start(bf16[16,128,128]{2,1,0:T(8,128)(2,1)} %get-tuple-element.11), channel_id=1, source_target_pairs={{0,1},{1,0},{2,3},{3,2},{4,5},{5,4},{6,7},{7,6},{8,9},{9,8},{10,11... | collective-permute-start | bytes 1572872 | tf_op jit(solution)/shard_map/ppermute | solution.py:308
  80.8 1.7 %collective-permute-done.4 = bf16[16,128,128]{2,1,0:T(8,128)(2,1)S(1)} collective-permute-done((bf16[16,128,128]{2,1,0:T(8,128)(2,1)}, bf16[16,128,128]{2,1,0:T(8,128)(2,1)S(1)}, u32[]{:S(2)}, u32[]{:S(2)}) %collective-permute-start.4) | collective-permute-done | bytes 524320 | tf_op jit(solution)/shard_map/ppermute | solution.py:308
  82.5 0.9 add_convert_fusion
  83.5 3.7 %all-to-all-start.1 = ((bf16[16,128,128]{2,1,0:T(8,128)(2,1)}), bf16[16,128,128]{2,1,0:T(8,128)(2,1)S(1)}, u32[]{:S(2)}, u32[]{:S(2)}) async-start(bf16[16,128,128]{2,1,0:T(8,128)(2,1)} %add_convert_fusion), calls=%async_computation.1 | async-start | bytes 1048576 | tf_op jit(solution)/shard_map/all_to_all | solution.py:312
  87.2 3.7 %collective-permute-start.6 = (bf16[128,1024]{1,0:T(8,128)(2,1)S(1)}, bf16[128,1024]{1,0:T(8,128)(2,1)S(1)}, u32[]{:S(2)}, u32[]{:S(2)}) collective-permute-start(bf16[128,1024]{1,0:T(8,128)(2,1)S(1)} %broadcast_select_fusion), channel_id=1, source_target_pairs={{0,224},{1,225},{2,226},{3,227},{4,228},{5,229},{6,230},{7,231},{8... | collective-permute-start | bytes 786440 | tf_op jit(solution)/shard_map/ppermute | solution.py:333
  90.9 4.1 %collective-permute-start.5 = (bf16[64,1024]{1,0:T(8,128)(2,1)S(1)}, bf16[64,1024]{1,0:T(8,128)(2,1)S(1)}, u32[]{:S(2)}, u32[]{:S(2)}) collective-permute-start(bf16[64,1024]{1,0:T(8,128)(2,1)S(1)} %get-tuple-element.14), channel_id=1, source_target_pairs={{0,225},{1,226},{2,227},{3,228},{4,229},{5,230},{6,231},{7,232},{8... | collective-permute-start | bytes 393224 | tf_op jit(solution)/shard_map/ppermute | solution.py:333
  95.0 1.9 %collective-permute-start.7 = (bf16[64,1024]{1,0:T(8,128)(2,1)S(1)}, bf16[64,1024]{1,0:T(8,128)(2,1)S(1)}, u32[]{:S(2)}, u32[]{:S(2)}) collective-permute-start(bf16[64,1024]{1,0:T(8,128)(2,1)S(1)} %get-tuple-element.13), channel_id=1, source_target_pairs={{1,224},{2,225},{3,226},{4,227},{5,228},{6,229},{7,230},{8,231},{9... | collective-permute-start | bytes 393224 | tf_op jit(solution)/shard_map/ppermute | solution.py:333
  96.9 8.1 %collective-permute-done.5.low_ref = bf16[64,1024]{1,0:T(8,128)(2,1)S(1)} collective-permute-done((bf16[64,1024]{1,0:T(8,128)(2,1)S(1)}, bf16[64,1024]{1,0:T(8,128)(2,1)S(1)}, u32[]{:S(2)}, u32[]{:S(2)}) %collective-permute-start.5) | collective-permute-done | bytes 131104 | tf_op jit(solution)/shard_map/ppermute | solution.py:333
  105.0 0.0 collective-permute-done.7.high_ref
  105.0 2.0 %shard_map.84.conv_ref = f32[128,1024]{1,0:T(8,128)S(1)} custom-call(bf16[64,1024]{1,0:T(8,128)(2,1)S(1)} %collective-permute-done.5.low_ref, bf16[128,1024]{1,0:T(8,128)(2,1)S(1)} %collective-permute-done.6.rows_ref, bf16[64,1024]{1,0:T(8,128)(2,1)S(1)} %collective-permute-done.7.high_ref, bf16[27,128,128]{2,1,0:T(8,128)(2,1)S(1)} %bitcast.9), custom_call_target="tpu_custom_call" | custom-call | flops 905969664 | bytes 1048576 | tf_op jit(solution)/shard_map/pallas_call | solution.py:296
  107.0 0.8 copy-done
  107.8 0.0 all-to-all-done.1.parts_ref
  107.8 0.8 copy-done.3
  108.6 2.5 %shard_map.85 = bf16[128,1024]{1,0:T(8,128)(2,1)} custom-call(s32[1,128]{1,0:T(1,128)} %times_ref.3, bf16[16,128,128]{2,1,0:T(8,128)(2,1)} %copy-done.3, f32[128,1024]{1,0:T(8,128)} %copy-done), custom_call_target="tpu_custom_call" | custom-call | flops 33554432 | bytes 1048576 | tf_op jit(solution)/shard_map/pallas_call | solution.py:218
  (23 shorter events, 0.1 us)
Async XLA Ops:
  34.4 15.0 %copy-start.2 = (bf16[8,400,128]{2,1,0:T(8,128)(2,1)}, bf16[8,400,128]{2,1,0:T(8,128)(2,1)S(1)}, u32[]{:S(2)}) copy-start(bf16[8,400,128]{2,1,0:T(8,128)(2,1)S(1)} %all_to_all.10.acts_a) | copy-start | bytes 2457604
  34.4 9.2 %collective-permute-start = (bf16[8,144,128]{2,1,0:T(8,128)(2,1)S(1)}, bf16[8,144,128]{2,1,0:T(8,128)(2,1)S(1)}, u32[]{:S(2)}, u32[]{:S(2)}) collective-permute-start(bf16[8,144,128]{2,1,0:T(8,128)(2,1)S(1)} %slice.16), channel_id=1, source_target_pairs={{0,16},{16,0},{1,17},{17,1},{2,18},{18,2},{3,19},{19,3},{4,20},{20... | collective-permute-start | bytes 884744 | tf_op jit(solution)/shard_map/ppermute | solution.py:308
  35.8 13.6 %collective-permute-start.1 = (bf16[8,144,128]{2,1,0:T(8,128)(2,1)S(1)}, bf16[8,144,128]{2,1,0:T(8,128)(2,1)S(1)}, u32[]{:S(2)}, u32[]{:S(2)}) collective-permute-start(bf16[8,144,128]{2,1,0:T(8,128)(2,1)S(1)} %slice.16), channel_id=1, source_target_pairs={{0,1},{1,0},{2,3},{3,2},{4,5},{5,4},{6,7},{7,6},{8,9},{9,8},{10,11... | collective-permute-start | bytes 884744 | tf_op jit(solution)/shard_map/ppermute | solution.py:308
  38.8 10.6 %collective-permute-start.3 = (bf16[8,128,128]{2,1,0:T(8,128)(2,1)S(1)}, bf16[8,128,128]{2,1,0:T(8,128)(2,1)S(1)}, u32[]{:S(2)}, u32[]{:S(2)}) collective-permute-start(bf16[8,128,128]{2,1,0:T(8,128)(2,1)S(1)} %slice.17), channel_id=1, source_target_pairs={{0,224},{1,225},{2,226},{3,227},{4,228},{5,229},{6,230},{7,231},{8... | collective-permute-start | bytes 786440 | tf_op jit(solution)/shard_map/ppermute | solution.py:333
  43.6 5.8 %copy-start.7 = (bf16[8,144,128]{2,1,0:T(8,128)(2,1)}, bf16[8,144,128]{2,1,0:T(8,128)(2,1)S(1)}, u32[]{:S(2)}) copy-start(bf16[8,144,128]{2,1,0:T(8,128)(2,1)S(1)} %collective-permute-done.acts_b) | copy-start | bytes 884740
  43.6 5.7 %collective-permute-start.2 = (bf16[8,144,128]{2,1,0:T(8,128)(2,1)S(1)}, bf16[8,144,128]{2,1,0:T(8,128)(2,1)S(1)}, u32[]{:S(2)}, u32[]{:S(2)}) collective-permute-start(bf16[8,144,128]{2,1,0:T(8,128)(2,1)S(1)} %collective-permute-done.acts_b), channel_id=1, source_target_pairs={{0,1},{1,0},{2,3},{3,2},{4,5},{5,4},{6,7},{7,6},{8,9},{9,8},{10,11... | collective-permute-start | bytes 884744 | tf_op jit(solution)/shard_map/ppermute | solution.py:308
  45.5 35.3 %copy-start.4 = (bf16[1,128,1024]{2,1,0:T(8,128)(2,1)S(1)}, bf16[1,128,1024]{2,1,0:T(8,128)(2,1)}, u32[]{:S(2)}) copy-start(bf16[1,128,1024]{2,1,0:T(8,128)(2,1)} %param.14) | copy-start | bytes 786436
  45.5 35.3 %copy-start.5 = (bf16[128,1024]{1,0:T(8,128)(2,1)S(1)}, bf16[128,1024]{1,0:T(8,128)(2,1)}, u32[]{:S(2)}) copy-start(bf16[128,1024]{1,0:T(8,128)(2,1)} %loss_ref.1) | copy-start | bytes 786436
  49.4 0.7 copy-start.10
  49.4 0.8 copy-start.8
  50.2 0.7 copy-start.9
  78.2 4.3 %copy-start.6 = (bf16[16,128,128]{2,1,0:T(8,128)(2,1)S(1)}, bf16[16,128,128]{2,1,0:T(8,128)(2,1)}, u32[]{:S(2)}) copy-start(bf16[16,128,128]{2,1,0:T(8,128)(2,1)} %get-tuple-element.10) | copy-start | bytes 1572868
  78.2 4.3 %collective-permute-start.4 = (bf16[16,128,128]{2,1,0:T(8,128)(2,1)}, bf16[16,128,128]{2,1,0:T(8,128)(2,1)S(1)}, u32[]{:S(2)}, u32[]{:S(2)}) collective-permute-start(bf16[16,128,128]{2,1,0:T(8,128)(2,1)} %get-tuple-element.11), channel_id=1, source_target_pairs={{0,1},{1,0},{2,3},{3,2},{4,5},{5,4},{6,7},{7,6},{8,9},{9,8},{10,11... | collective-permute-start | bytes 1572872 | tf_op jit(solution)/shard_map/ppermute | solution.py:308
  83.5 21.5 %copy-start.1 = (bf16[1,27,128,128]{3,2,1,0:T(8,128)(2,1)S(1)}, bf16[1,27,128,128]{3,2,1,0:T(8,128)(2,1)}, u32[]{:S(2)}) copy-start(bf16[1,27,128,128]{3,2,1,0:T(8,128)(2,1)} %param.13) | copy-start | bytes 2654212
  83.5 24.4 %all-to-all-start.1 = ((bf16[16,128,128]{2,1,0:T(8,128)(2,1)}), bf16[16,128,128]{2,1,0:T(8,128)(2,1)S(1)}, u32[]{:S(2)}, u32[]{:S(2)}) async-start(bf16[16,128,128]{2,1,0:T(8,128)(2,1)} %add_convert_fusion), calls=%async_computation.1 | async-start | bytes 1048576 | tf_op jit(solution)/shard_map/all_to_all | solution.py:312
  87.2 17.8 %collective-permute-start.6 = (bf16[128,1024]{1,0:T(8,128)(2,1)S(1)}, bf16[128,1024]{1,0:T(8,128)(2,1)S(1)}, u32[]{:S(2)}, u32[]{:S(2)}) collective-permute-start(bf16[128,1024]{1,0:T(8,128)(2,1)S(1)} %broadcast_select_fusion), channel_id=1, source_target_pairs={{0,224},{1,225},{2,226},{3,227},{4,228},{5,229},{6,230},{7,231},{8... | collective-permute-start | bytes 786440 | tf_op jit(solution)/shard_map/ppermute | solution.py:333
  90.9 14.1 %collective-permute-start.5 = (bf16[64,1024]{1,0:T(8,128)(2,1)S(1)}, bf16[64,1024]{1,0:T(8,128)(2,1)S(1)}, u32[]{:S(2)}, u32[]{:S(2)}) collective-permute-start(bf16[64,1024]{1,0:T(8,128)(2,1)S(1)} %get-tuple-element.14), channel_id=1, source_target_pairs={{0,225},{1,226},{2,227},{3,228},{4,229},{5,230},{6,231},{7,232},{8... | collective-permute-start | bytes 393224 | tf_op jit(solution)/shard_map/ppermute | solution.py:333
  95.0 10.0 %collective-permute-start.7 = (bf16[64,1024]{1,0:T(8,128)(2,1)S(1)}, bf16[64,1024]{1,0:T(8,128)(2,1)S(1)}, u32[]{:S(2)}, u32[]{:S(2)}) collective-permute-start(bf16[64,1024]{1,0:T(8,128)(2,1)S(1)} %get-tuple-element.13), channel_id=1, source_target_pairs={{1,224},{2,225},{3,226},{4,227},{5,228},{6,229},{7,230},{8,231},{9... | collective-permute-start | bytes 393224 | tf_op jit(solution)/shard_map/ppermute | solution.py:333
  107.0 0.8 copy-start
  107.8 0.8 copy-start.3
